TPU v7x, 768 devices: a whole 4x8x12 slice. The times are simulated.
768 devices in a mesh: blk: 96 (over x, z_lo, y), grp: 8 (over z_hi, core).
Axes of the slice: x: 4, y: 8, z: 12 (z_hi: 4, z_lo: 3; z = z_hi * 3 + z_lo), core: 2. Of those that a mesh axis runs over, the one named last changes fastest.
Arguments:
- image: bfloat16 [196608, 1152], P(('blk', 'grp')), may hold values from -0.35355339 to 0.35355339
- text: bfloat16 [196608, 1152], P(('blk', 'grp')), may hold values from -0.35355339 to 0.35355339
- exponent_of_multiplier: float32 [1], replicated, may hold values from 4.4 to 4.7
- bias: float32 [1], replicated, may hold values from -13 to -11
Outputs:
- grad_image: float32 [196608, 1152], P(('blk', 'grp'))
- grad_text: float32 [196608, 1152], P(('blk', 'grp'))
- totals: float32 [3], replicated
All inputs are finite; a program needn't handle non-finite values.
Results may differ from a plain program's by a relative error of at most 0.0039.
The roundings to bfloat16 on the way count: a program that leaves them out, or rounds other values in their place, can miss the bound.
Values may be sent and summed in bfloat16 or wider, within the bound.
No kernel may reach another device: no remote copies, remote signals or barrier semaphores. Data moves between devices by JAX's collectives and lax.ppermute only.
A program may use at most 32 MiB of HBM per device.

v0:
```python
import jax
import jax.numpy as jnp
from jax import lax
from jax.sharding import PartitionSpec as P

STEPS = 4


epsilon = 1e-06


def passed_along(value, axis, steps):
    count = lax.axis_size(axis)
    pairs = [(source, (source + steps) % count) for source in range(count)]
    return lax.ppermute(value, axis, pairs)


def to_unit(values):
    valuef = values.astype(jnp.float32)
    inverse = lax.rsqrt(jnp.sum(valuef * valuef, axis=-1, keepdims=True) + epsilon)
    return (valuef * inverse, inverse)


def couple_derivatives(
    upper_entries, lower_entries, sharpness_factor, offset_amount, desired_polarity
):
    cosine_grid = lax.dot_general(
        upper_entries, lower_entries, (((1,), (1,)), ((), ())), preferred_element_type=jnp.float32
    )
    pair_score_grid = sharpness_factor * cosine_grid + offset_amount
    logistic_derivatives = -desired_polarity * jax.nn.sigmoid(-desired_polarity * pair_score_grid)
    return (cosine_grid, pair_score_grid, logistic_derivatives)


def body(image, text, exponent_of_multiplier, bias):
    img_unit, img_inverse = to_unit(image)
    txt_unit, txt_inverse = to_unit(text)
    photo_portion = img_unit.astype(jnp.bfloat16)
    kept_caption = txt_unit.astype(jnp.bfloat16)
    row_count = image.shape[0]
    sharpness_factor = jnp.exp(exponent_of_multiplier[0])
    offset_amount = bias[0]
    diagonal_mask = jnp.eye(row_count, dtype=jnp.float32)
    photo_derivative = jnp.zeros(image.shape, jnp.float32)
    text_grad = jnp.zeros(text.shape, jnp.float32)
    loss_sum = jnp.float32(0.0)
    multiplier_accumulated = jnp.float32(0.0)
    bias_sum = jnp.float32(0.0)
    for cycle_step in range(STEPS):
        if cycle_step == 0:
            desired_polarity = 2.0 * diagonal_mask - 1.0
        else:
            desired_polarity = -jnp.ones((row_count, row_count), jnp.float32)
        cosine_grid, pair_score_grid, logistic_derivatives = couple_derivatives(
            photo_portion, kept_caption, sharpness_factor, offset_amount, desired_polarity
        )
        loss_sum = loss_sum + jnp.sum(jax.nn.softplus(-desired_polarity * pair_score_grid))
        multiplier_accumulated = multiplier_accumulated + sharpness_factor * jnp.sum(
            logistic_derivatives * cosine_grid
        )
        bias_sum = bias_sum + jnp.sum(logistic_derivatives)
        midpoint_steepness = logistic_derivatives.astype(jnp.bfloat16)
        photo_derivative = photo_derivative + sharpness_factor * jnp.dot(
            midpoint_steepness, kept_caption, preferred_element_type=jnp.float32
        )
        segment_share = sharpness_factor * lax.dot_general(
            midpoint_steepness,
            photo_portion,
            (((0,), (0,)), ((), ())),
            preferred_element_type=jnp.float32,
        )
        text_grad = text_grad + segment_share
        if cycle_step + 1 < STEPS:
            text_grad = passed_along(text_grad, "blk", 1)
        if cycle_step + 1 < STEPS:
            kept_caption = passed_along(kept_caption, "blk", 1)
    text_grad = passed_along(text_grad, "blk", -(STEPS - 1))
    loss_all, scale_all, bias_all = lax.psum(
        (loss_sum, multiplier_accumulated, bias_sum), ("blk", "grp")
    )
    pair_count = jnp.float32(row_count * lax.axis_size("blk") * lax.axis_size("grp"))
    totals = jnp.stack([loss_all, scale_all, bias_all]) / pair_count
    grad_image = img_inverse * (
        photo_derivative - img_unit * jnp.sum(img_unit * photo_derivative, axis=-1, keepdims=True)
    )
    grad_text = txt_inverse * (
        text_grad - txt_unit * jnp.sum(txt_unit * text_grad, axis=-1, keepdims=True)
    )
    return (grad_image, grad_text, totals)


def solution(mesh):
    placed = (P(("blk", "grp"), None), P(("blk", "grp"), None), P(), P())
    return jax.shard_map(
        body,
        mesh=mesh,
        in_specs=placed,
        out_specs=(P(("blk", "grp"), None), P(("blk", "grp"), None), P()),
        check_vma=False,
    )
```

profile of v0, /device:TPU:33, one launch (start us, length us, event | category | flops | bytes accessed | tf_op | source)
XLA Modules:
  0.0 368.0 jit_solution(7116385459301346847)
XLA Ops:
  0.7 1.4 fusion.11
  2.7 1.3 fusion.15
  4.8 1.3 fusion.16
  6.5 2.3 collective-permute-start.3
  8.9 2.3 collective-permute-start
  11.2 37.9 %collective-permute-done = bf16[256,1152]{1,0:T(8,128)(2,1)S(1)} collective-permute-done((bf16[256,1152]{1,0:T(8,128)(2,1)S(1)}, bf16[256,1152]{1,0:T(8,128)(2,1)S(1)}, u32[]{:S(2)}, u32[]{:S(2)}) %collective-permute-start) | collective-permute-done | bytes 589856 | tf_op jit(solution)/shard_map/ppermute | solution.py:15
  51.1 1.9 collective-permute-start.4
  53.0 1.9 collective-permute-start.1
  54.9 37.9 %collective-permute-done.1 = bf16[256,1152]{1,0:T(8,128)(2,1)} collective-permute-done((bf16[256,1152]{1,0:T(8,128)(2,1)S(1)}, bf16[256,1152]{1,0:T(8,128)(2,1)}, u32[]{:S(2)}, u32[]{:S(2)}) %collective-permute-start.1) | collective-permute-done | bytes 589856 | tf_op jit(solution)/shard_map/ppermute | solution.py:15
  92.8 2.3 fusion.18
  95.9 1.9 collective-permute-start.5
  97.8 1.9 collective-permute-start.2
  99.8 1.4 fusion.27
  105.0 1.9 convolution_add_fusion.2
  108.7 28.0 %collective-permute-done.2 = bf16[256,1152]{1,0:T(8,128)(2,1)} collective-permute-done((bf16[256,1152]{1,0:T(8,128)(2,1)}, bf16[256,1152]{1,0:T(8,128)(2,1)}, u32[]{:S(2)}, u32[]{:S(2)}) %collective-permute-start.2) | collective-permute-done | bytes 589856 | tf_op jit(solution)/shard_map/ppermute | solution.py:15
  136.7 2.3 fusion.19
  139.7 2.4 add.127
  142.2 1.9 collective-permute-start.6
  144.1 2.4 convolution_add_fusion.1
  148.5 212.3 %all-reduce = (f32[1]{0:T(128)}, f32[1]{0:T(128)}, f32[1]{0:T(128)}) all-reduce(f32[1]{0:T(128)} %bitcast.4, f32[1]{0:T(128)} %bitcast.3, f32[1]{0:T(128)} %bitcast.2), channel_id=1, replica_groups=mesh['blk'=96,'grp'=8] {'blk','grp'}, use_global_device_ids=true, to_apply=%region_18.19 | all-reduce | flops 3 | bytes 24 | tf_op jit(solution)/shard_map/psum | solution.py:78
  360.7 2.4 maximum_multiply_fusion
  363.1 2.0 fusion.8
  365.1 1.3 fusion.10
  366.7 1.3 fusion.14
  (28 shorter events, 4.4 us)
Async XLA Ops:
  0.6 4.2 %copy-start = (bf16[256,1152]{1,0:T(8,128)(2,1)S(1)}, bf16[256,1152]{1,0:T(8,128)(2,1)}, u32[]{:S(2)}) copy-start(bf16[256,1152]{1,0:T(8,128)(2,1)} %param.4) | copy-start | bytes 1769476
  0.6 3.3 copy-start.1
  6.5 43.8 %collective-permute-start.3 = (f32[256,1152]{1,0:T(8,128)S(1)}, f32[256,1152]{1,0:T(8,128)S(1)}, u32[]{:S(2)}, u32[]{:S(2)}) collective-permute-start(f32[256,1152]{1,0:T(8,128)S(1)} %convolution_multiply_fusion.3), channel_id=1, source_target_pairs={{0,8},{8,16},{16,24},{24,32},{32,40},{40,48},{48,56},{56,64},{64,7... | collective-permute-start | bytes 3538952 | tf_op jit(solution)/shard_map/ppermute | solution.py:15
  8.9 40.3 %collective-permute-start = (bf16[256,1152]{1,0:T(8,128)(2,1)S(1)}, bf16[256,1152]{1,0:T(8,128)(2,1)S(1)}, u32[]{:S(2)}, u32[]{:S(2)}) collective-permute-start(bf16[256,1152]{1,0:T(8,128)(2,1)S(1)} %fusion.4), channel_id=1, source_target_pairs={{0,8},{8,16},{16,24},{24,32},{32,40},{40,48},{48,56},{56,64},{64,7... | collective-permute-start | bytes 1769480 | tf_op jit(solution)/shard_map/ppermute | solution.py:15
  49.1 3.9 %copy-start.3 = (bf16[256,1152]{1,0:T(8,128)(2,1)}, bf16[256,1152]{1,0:T(8,128)(2,1)S(1)}, u32[]{:S(2)}) copy-start(bf16[256,1152]{1,0:T(8,128)(2,1)S(1)} %collective-permute-done) | copy-start | bytes 1769476
  50.4 0.7 copy-start.2
  51.1 44.7 %collective-permute-start.4 = (f32[256,1152]{1,0:T(8,128)S(1)}, f32[256,1152]{1,0:T(8,128)S(1)}, u32[]{:S(2)}, u32[]{:S(2)}) collective-permute-start(f32[256,1152]{1,0:T(8,128)S(1)} %fusion.1), channel_id=1, source_target_pairs={{0,8},{8,16},{16,24},{24,32},{32,40},{40,48},{48,56},{56,64},{64,7... | collective-permute-start | bytes 3538952 | tf_op jit(solution)/shard_map/ppermute | solution.py:15
  53.0 39.8 %collective-permute-start.1 = (bf16[256,1152]{1,0:T(8,128)(2,1)S(1)}, bf16[256,1152]{1,0:T(8,128)(2,1)}, u32[]{:S(2)}, u32[]{:S(2)}) collective-permute-start(bf16[256,1152]{1,0:T(8,128)(2,1)S(1)} %collective-permute-done), channel_id=1, source_target_pairs={{0,8},{8,16},{16,24},{24,32},{32,40},{40,48},{48,56},{56,64},{64,7... | collective-permute-start | bytes 1769480 | tf_op jit(solution)/shard_map/ppermute | solution.py:15
  95.1 0.7 copy-start.4
  95.9 43.9 %collective-permute-start.5 = (f32[256,1152]{1,0:T(8,128)S(1)}, f32[256,1152]{1,0:T(8,128)}, u32[]{:S(2)}, u32[]{:S(2)}) collective-permute-start(f32[256,1152]{1,0:T(8,128)S(1)} %add.126), channel_id=1, source_target_pairs={{0,8},{8,16},{16,24},{24,32},{32,40},{40,48},{48,56},{56,64},{64,7... | collective-permute-start | bytes 3538952 | tf_op jit(solution)/shard_map/ppermute | solution.py:15
  97.8 38.9 %collective-permute-start.2 = (bf16[256,1152]{1,0:T(8,128)(2,1)}, bf16[256,1152]{1,0:T(8,128)(2,1)}, u32[]{:S(2)}, u32[]{:S(2)}) collective-permute-start(bf16[256,1152]{1,0:T(8,128)(2,1)} %collective-permute-done.1), channel_id=1, source_target_pairs={{0,8},{8,16},{16,24},{24,32},{32,40},{40,48},{48,56},{56,64},{64,7... | collective-permute-start | bytes 1769480 | tf_op jit(solution)/shard_map/ppermute | solution.py:15
  139.0 0.7 copy-start.6
  139.7 4.4 %copy-start.5 = (f32[256,256]{1,0:T(8,128)S(1)}, f32[256,256]{1,0:T(8,128)}, u32[]{:S(2)}) copy-start(f32[256,256]{1,0:T(8,128)} %copy-done.4) | copy-start | bytes 786436
  142.2 224.2 %collective-permute-start.6 = (f32[256,1152]{1,0:T(8,128)}, f32[256,1152]{1,0:T(8,128)S(1)}, u32[]{:S(2)}, u32[]{:S(2)}) collective-permute-start(f32[256,1152]{1,0:T(8,128)} %add.127), channel_id=1, source_target_pairs={{0,744},{8,752},{16,760},{24,0},{32,8},{40,16},{48,24},{56,32},{64... | collective-permute-start | bytes 3538952 | tf_op jit(solution)/shard_map/ppermute | solution.py:15
where the time goes:
time: 369 us; the launch traced here: 368 us
  blocking collectives  212 us (57%)
  waiting for transfers between devices  104 us (28%)
  matrix products  16.5 us (4%)
  starting transfers between devices  14.2 us (4%)
  other arithmetic  10.6 us (3%)
  between operations  9.7 us (3%)
    psum x1, blocking collectives, body(): lax.psum((loss_sum, multiplier_accumulated, bias_sum), ('blk', 'grp'))  212 us
    ppermute x7, waiting for transfers between devices, passed_along(): return lax.ppermute(value, axis, pairs)  104 us
    ppermute x7, starting transfers between devices, passed_along(): return lax.ppermute(value, axis, pairs)  14.2 us
    dot_general x4, matrix products, body(): jnp.dot(midpoint_steepness, kept_caption, preferred_element_type=jnp.floa...  7.75 us
  transfers between devices with their start and end apart: 7, of which 3 were waited for; matrix products, arithmetic and copies ran while one was open for 5% of the time, Pallas kernels for 0%

commit v1 on v0

v1 whole, which is shorter than its diff:
```python
import jax
import jax.numpy as jnp
from jax import lax
from jax.sharding import Mesh, PartitionSpec as P

EPSILON = 1e-06
BLK_PARTS = (4, 3, 8)
GRP_PARTS = (4, 2)
AXES = ("x", "l", "y", "h", "c")


def hop(value, steps):
    n_blk, n_grp = 96, 8
    pairs = []
    for b in range(n_blk):
        for g in range(n_grp):
            way = steps if g % 2 == 0 else -steps
            pairs.append((b * n_grp + g, ((b + way) % n_blk) * n_grp + g))
    return lax.ppermute(value, AXES, pairs)


def to_unit(values):
    valuef = values.astype(jnp.float32)
    inverse = lax.rsqrt(jnp.sum(valuef * valuef, axis=-1, keepdims=True) + EPSILON)
    return valuef * inverse, inverse


def grid_of(rows, cols):
    return lax.dot_general(rows, cols, (((1,), (1,)), ((), ())), preferred_element_type=jnp.float32)


def slope_of(cosine, scale, offset, z):
    return -z * jax.nn.sigmoid(-z * (scale * cosine + offset))


def sums_of(cosine, scale, offset, z):
    logit = scale * cosine + offset
    slope = -z * jax.nn.sigmoid(-z * logit)
    return jnp.sum(jax.nn.softplus(-z * logit)), jnp.sum(slope * cosine), jnp.sum(slope)


def add3(a, b):
    return tuple(x + y for x, y in zip(a, b))


def summed(value, axes, count):
    out = jnp.broadcast_to(value.reshape(1, 1, 128), (count, 1, 128))
    return jnp.sum(lax.all_to_all(out, axes, 0, 0, tiled=True), axis=0)


def body(image, text, exponent_of_multiplier, bias):
    bar = lax.optimization_barrier
    scale = jnp.exp(exponent_of_multiplier[0])
    offset = bias[0]
    rows = image.shape[0]
    even = lax.axis_index("c") == 0
    p_raw = jnp.where(even, text, image)
    q_raw = jnp.where(even, image, text)
    p_unit, p_inv = to_unit(p_raw)
    p0 = p_unit.astype(jnp.bfloat16)
    p1 = hop(p0, 1)
    q_unit, q_inv = to_unit(q_raw)
    q0 = q_unit.astype(jnp.bfloat16)
    q1 = hop(q0, -1)
    z0 = 2.0 * jnp.eye(rows, dtype=jnp.float32) - 1.0
    z = jnp.float32(-1.0)

    s00 = grid_of(q0, p0)
    sums = sums_of(s00, scale, offset, z0)
    d00 = slope_of(s00, scale, offset, z0).astype(jnp.bfloat16)
    g_q = jnp.dot(d00, p0, preferred_element_type=jnp.float32)
    g_p = lax.dot_general(d00, q0, (((0,), (0,)), ((), ())), preferred_element_type=jnp.float32)
    sums, g_q, g_p, p1, q1 = bar((sums, g_q, g_p, p1, q1))

    p2 = hop(p1, 1)
    s01 = grid_of(q0, p1)
    sums = add3(sums, sums_of(s01, scale, offset, z))
    d01 = slope_of(s01, scale, offset, z).astype(jnp.bfloat16)
    sums = add3(sums, sums_of(grid_of(q1, p1), scale, offset, z))
    d10 = slope_of(grid_of(p0, q1), scale, offset, z).astype(jnp.bfloat16)
    g_q = g_q + jnp.dot(d01, p1, preferred_element_type=jnp.float32)
    g_p = g_p + jnp.dot(d10, q1, preferred_element_type=jnp.float32)
    sums, g_q, g_p, q1s = bar((sums, g_q, g_p, q1))
    q2 = hop(q1s, -1)

    sums = add3(sums, sums_of(grid_of(q1, p2), scale, offset, z))
    sums, p2s = bar((sums, p2))
    p3 = hop(p2s, 1)
    loss, by_scale, by_bias = sums
    row = jnp.concatenate([jnp.stack([loss, scale * by_scale, by_bias]), jnp.zeros((125,), jnp.float32)])
    row = summed(row, ("x", "y", "c"), 64)
    row, q2 = bar((row, q2))
    q3 = hop(q2, -1)
    row, q3, p3 = bar((summed(row, ("l", "h"), 12), q3, p3))
    pair_count = jnp.float32(rows * 768)
    totals = row.reshape(128)[:3] / pair_count

    d02 = slope_of(grid_of(q0, p2), scale, offset, z).astype(jnp.bfloat16)
    d20 = slope_of(grid_of(p0, q2), scale, offset, z).astype(jnp.bfloat16)
    d03 = slope_of(grid_of(q0, p3), scale, offset, z).astype(jnp.bfloat16)
    d30 = slope_of(grid_of(p0, q3), scale, offset, z).astype(jnp.bfloat16)
    g_q = g_q + jnp.dot(d02, p2, preferred_element_type=jnp.float32)
    g_p = g_p + jnp.dot(d20, q2, preferred_element_type=jnp.float32)
    g_q = g_q + jnp.dot(d03, p3, preferred_element_type=jnp.float32)
    g_p = g_p + jnp.dot(d30, q3, preferred_element_type=jnp.float32)
    g_q = scale * g_q
    g_p = scale * g_p
    grad_q = q_inv * (g_q - q_unit * jnp.sum(q_unit * g_q, axis=-1, keepdims=True))
    grad_p = p_inv * (g_p - p_unit * jnp.sum(p_unit * g_p, axis=-1, keepdims=True))
    return jnp.where(even, grad_q, grad_p), jnp.where(even, grad_p, grad_q), totals


def solution(mesh):
    fine = Mesh(mesh.devices.reshape(BLK_PARTS + GRP_PARTS), AXES)
    split = P(AXES, None)
    return jax.shard_map(
        body,
        mesh=fine,
        in_specs=(split, split, P(), P()),
        out_specs=(split, split, P()),
        check_vma=False,
    )
```

time: 369 us -> 124 us (0.34)
  the two profiles are of different devices: /device:TPU:33 before, /device:TPU:2 now
where the time goes in v1:
time: 124 us; the launch traced here: 123 us
  starting transfers between devices  42.4 us (34%)
  matrix products  29.8 us (24%)
  blocking collectives  19.8 us (16%)
  other arithmetic  11.1 us (9%)
  waiting for transfers between devices  9.9 us (8%)
  between operations  9.78 us (8%)
    ppermute x6, starting transfers between devices, hop(): return lax.ppermute(value, AXES, pairs)  26.5 us
    all_to_all x1, blocking collectives, summed(): return jnp.sum(lax.all_to_all(out, axes, 0, 0, tiled=True), axis=0)  19.8 us
    all_to_all x1, starting transfers between devices, summed(): return jnp.sum(lax.all_to_all(out, axes, 0, 0, tiled=True), axis=0)  15.8 us
    dot_general x4, matrix products, grid_of(): lax.dot_general(rows, cols, (((1,), (1,)), ((), ())), preferred_element_t...  8.55 us
    all_to_all x1, waiting for transfers between devices, summed(): return jnp.sum(lax.all_to_all(out, axes, 0, 0, tiled=True), axis=0)  5.07 us
    ppermute x6, waiting for transfers between devices, hop(): return lax.ppermute(value, AXES, pairs)  4.83 us
    dot_general x1, matrix products, body(): g_q = g_q + jnp.dot(d02, p2, preferred_element_type=jnp.float32)  3.68 us
    dot_general x1, matrix products, body(): g_p = g_p + jnp.dot(d20, q2, preferred_element_type=jnp.float32)  3.59 us
  transfers between devices with their start and end apart: 7, of which 3 were waited for; matrix products, arithmetic and copies ran while one was open for 17% of the time, Pallas kernels for 0%

profile of v1, /device:TPU:2, one launch (start us, length us, event | category | flops | bytes accessed | tf_op | source)
XLA Modules:
  0.0 123.4 jit_solution(7201317967170606505)
XLA Ops:
  0.6 1.8 %fusion.17 = (f32[256]{0:T(256)S(1)}, bf16[256,1152]{1,0:T(8,128)(2,1)S(1)}, f32[256]{0:T(256)S(1)}, bf16[256,1152]{1,0:T(8,128)(2,1)S(1)}) fusion(bf16[256,1152]{1,0:T(8,128)(2,1)} %param.5, bf16[256,1152]{1,0:T(8,128)(2,1)} %param.4, pred[]{:T(512)S(6)} %eq.8), kind=kLoop, calls=%fused_computation.23 | loop fusion | flops 2358784 | bytes 2361345 | tf_op jit(solution)/shard_map/reduce_sum | solution.py:24
  2.7 3.5 %collective-permute-start = (bf16[256,1152]{1,0:T(8,128)(2,1)S(1)}, bf16[256,1152]{1,0:T(8,128)(2,1)}, u32[]{:S(2)}, u32[]{:S(2)}) collective-permute-start(bf16[256,1152]{1,0:T(8,128)(2,1)S(1)} %fusion.6), channel_id=1, source_target_pairs={{0,8},{1,761},{2,10},{3,763},{4,12},{5,765},{6,14},{7,767},{8,16},... | collective-permute-start | bytes 1769480 | tf_op jit(solution)/shard_map/ppermute | solution.py:19
  6.3 7.4 %collective-permute-start.1 = (bf16[256,1152]{1,0:T(8,128)(2,1)S(1)}, bf16[256,1152]{1,0:T(8,128)(2,1)}, u32[]{:S(2)}, u32[]{:S(2)}) collective-permute-start(bf16[256,1152]{1,0:T(8,128)(2,1)S(1)} %fusion.9), channel_id=1, source_target_pairs={{0,760},{1,9},{2,762},{3,11},{4,764},{5,13},{6,766},{7,15},{8,0},{... | collective-permute-start | bytes 1769480 | tf_op jit(solution)/shard_map/ppermute | solution.py:19
  16.4 1.5 %fusion.76 = f32[256,1152]{1,0:T(8,128)} fusion(f32[256,256]{1,0:T(8,128)S(1)} %get-tuple-element.67, f32[]{:T(128)} %bitcast.32, f32[]{:T(128)} %bitcast, bf16[256,1152]{1,0:T(8,128)(2,1)S(1)} %get-tuple-element.66, f32[256]{0:T(256)S(1)} %add_rsqrt_fusion.1), kind=kOutput, calls=%fused_computation.107 | convolution fusion | flops 152666112 | bytes 2032648 | tf_op jit(solution)/shard_map/dot_general | solution.py:72
  17.9 1.5 %fusion.78 = f32[256,1152]{1,0:T(8,128)} fusion(f32[256,256]{1,0:T(8,128)S(1)} %get-tuple-element.67, f32[]{:T(128)} %bitcast.37, f32[]{:T(128)} %bitcast, bf16[256,1152]{1,0:T(8,128)(2,1)S(1)} %get-tuple-element.60, f32[256]{0:T(256)S(1)} %add_rsqrt_fusion), kind=kOutput, calls=%fused_computation.109 | convolution fusion | flops 152666112 | bytes 2032648 | tf_op jit(solution)/shard_map/dot_general | solution.py:71
  19.6 4.6 %collective-permute-done.1 = bf16[256,1152]{1,0:T(8,128)(2,1)} collective-permute-done((bf16[256,1152]{1,0:T(8,128)(2,1)S(1)}, bf16[256,1152]{1,0:T(8,128)(2,1)}, u32[]{:S(2)}, u32[]{:S(2)}) %collective-permute-start.1) | collective-permute-done | bytes 589856 | tf_op jit(solution)/shard_map/ppermute | solution.py:19
  24.2 1.9 %collective-permute-start.2 = (bf16[256,1152]{1,0:T(8,128)(2,1)}, bf16[256,1152]{1,0:T(8,128)(2,1)}, u32[]{:S(2)}, u32[]{:S(2)}) collective-permute-start(bf16[256,1152]{1,0:T(8,128)(2,1)} %collective-permute-done), channel_id=1, source_target_pairs={{0,8},{1,761},{2,10},{3,763},{4,12},{5,765},{6,14},{7,767},{8,16},... | collective-permute-start | bytes 1769480 | tf_op jit(solution)/shard_map/ppermute | solution.py:19
  26.1 2.3 %fusion.85 = (f32[]{:T(128)}, f32[]{:T(128)}, f32[]{:T(128)}, f32[256,256]{1,0:T(8,128)S(1)}) fusion(f32[]{:T(128)} %bitcast.28, f32[]{:T(128)} %bitcast, bf16[256,1152]{1,0:T(8,128)(2,1)} %collective-permute-done, bf16[256,1152]{1,0:T(8,128)(2,1)S(1)} %get-tuple-element.66, f32[256]{0:T(256)S(1)} %add_rsqrt_fusion.1), kind=kOutput, calls=%fused_computation.120 | convolution fusion | flops 152862720 | bytes 1442836 | tf_op jit(solution)/shard_map/dot_general | solution.py:29
  28.4 1.4 %fusion.59 = f32[256,1152]{1,0:T(8,128)S(1)} fusion(bf16[256,1152]{1,0:T(8,128)(2,1)} %collective-permute-done, f32[256,256]{1,0:T(8,128)S(1)} %get-tuple-element.68, f32[]{:T(128)} %bitcast.33, f32[]{:T(128)} %bitcast), kind=kOutput, calls=%fused_computation.90 | convolution fusion | flops 151388160 | bytes 2031624 | tf_op jit(solution)/shard_map/dot_general | solution.py:81
  29.8 2.5 %fusion.57 = (f32[]{:T(128)}, f32[]{:T(128)}, f32[]{:T(128)}) fusion(f32[]{:T(128)} %bitcast.30, f32[]{:T(128)} %bitcast, bf16[256,1152]{1,0:T(8,128)(2,1)} %collective-permute-done.1, bf16[256,1152]{1,0:T(8,128)(2,1)} %collective-permute-done), kind=kOutput, calls=%fused_computation.88 | convolution fusion | flops 151977984 | bytes 1179668 | tf_op jit(solution)/shard_map/dot_general | solution.py:29
  39.4 3.2 %fusion.50 = f32[256,1152]{1,0:T(8,128)} fusion(bf16[256,1152]{1,0:T(8,128)(2,1)} %collective-permute-done.1, f32[]{:T(128)} %bitcast.27, f32[]{:T(128)} %bitcast, bf16[256,1152]{1,0:T(8,128)(2,1)S(1)} %get-tuple-element.60, f32[256]{0:T(256)S(1)} %add_rsqrt_fusion), kind=kOutput, calls=%fused_computation.61 | convolution fusion | flops 303267840 | bytes 2360328 | tf_op jit(solution)/shard_map/dot_general | solution.py:82
  42.7 1.7 %add.167 = f32[256,1152]{1,0:T(8,128)S(1)} add(f32[256,1152]{1,0:T(8,128)} %fusion.76, f32[256,1152]{1,0:T(8,128)} %fusion.50) | non-fusion elementwise | flops 294912 | bytes 3538944 | tf_op jit(solution)/shard_map/add | solution.py:82
  44.4 8.4 %collective-permute-start.3 = (bf16[256,1152]{1,0:T(8,128)(2,1)}, bf16[256,1152]{1,0:T(8,128)(2,1)}, u32[]{:S(2)}, u32[]{:S(2)}) collective-permute-start(bf16[256,1152]{1,0:T(8,128)(2,1)} %collective-permute-done.1), channel_id=1, source_target_pairs={{0,760},{1,9},{2,762},{3,11},{4,764},{5,13},{6,766},{7,15},{8,0},{... | collective-permute-start | bytes 1769480 | tf_op jit(solution)/shard_map/ppermute | solution.py:19
  52.9 2.4 %fusion.58 = (f32[]{:T(128)}, f32[]{:T(128)}, f32[]{:T(128)}) fusion(f32[]{:T(128)} %bitcast.29, f32[]{:T(128)} %bitcast, bf16[256,1152]{1,0:T(8,128)(2,1)} %collective-permute-done.1, bf16[256,1152]{1,0:T(8,128)(2,1)} %collective-permute-done.2), kind=kOutput, calls=%fused_computation.89 | convolution fusion | flops 151977984 | bytes 1179668 | tf_op jit(solution)/shard_map/dot_general | solution.py:29
  57.9 15.8 %all-to-all-start = ((f32[64,1,128]{2,1,0:T(1,128)}), f32[64,1,128]{2,1,0:T(1,128)}, u32[]{:S(2)}, u32[]{:S(2)}) async-start(f32[64,1,128]{2,1,0:T(1,128)} %broadcast_in_dim.9), calls=%async_computation | async-start | bytes 65536 | tf_op jit(solution)/shard_map/all_to_all | solution.py:48
  73.8 3.4 %collective-permute-start.5 = (bf16[256,1152]{1,0:T(8,128)(2,1)}, bf16[256,1152]{1,0:T(8,128)(2,1)}, u32[]{:S(2)}, u32[]{:S(2)}) collective-permute-start(bf16[256,1152]{1,0:T(8,128)(2,1)} %collective-permute-done.2), channel_id=1, source_target_pairs={{0,8},{1,761},{2,10},{3,763},{4,12},{5,765},{6,14},{7,767},{8,16},... | collective-permute-start | bytes 1769480 | tf_op jit(solution)/shard_map/ppermute | solution.py:19
  77.2 5.1 %all-to-all-done = f32[64,1,128]{2,1,0:T(1,128)} async-done(((f32[64,1,128]{2,1,0:T(1,128)}), f32[64,1,128]{2,1,0:T(1,128)}, u32[]{:S(2)}, u32[]{:S(2)}) %all-to-all-start) | async-done | bytes 32800 | tf_op jit(solution)/shard_map/all_to_all | solution.py:48
  83.0 1.9 %collective-permute-start.4 = (bf16[256,1152]{1,0:T(8,128)(2,1)}, bf16[256,1152]{1,0:T(8,128)(2,1)}, u32[]{:S(2)}, u32[]{:S(2)}) collective-permute-start(bf16[256,1152]{1,0:T(8,128)(2,1)} %collective-permute-done.3), channel_id=1, source_target_pairs={{0,760},{1,9},{2,762},{3,11},{4,764},{5,13},{6,766},{7,15},{8,0},{... | collective-permute-start | bytes 1769480 | tf_op jit(solution)/shard_map/ppermute | solution.py:19
  85.0 19.8 %all_to_all.10 = f32[12,1,128]{2,1,0:T(1,128)S(1)} all-to-all(f32[12,1,128]{2,1,0:T(1,128)S(1)} %broadcast_in_dim.22), channel_id=1, replica_groups=mesh['x'=4,'l'=3,'y'=8,'h'=4,'c'=2] {'l','h'}, dimensions={0} | all-to-all | bytes 12288 | tf_op jit(solution)/shard_map/all_to_all | solution.py:48
  106.5 3.2 %fusion.49 = f32[256,1152]{1,0:T(8,128)} fusion(bf16[256,1152]{1,0:T(8,128)(2,1)} %collective-permute-done.5, f32[]{:T(128)} %bitcast.36, f32[]{:T(128)} %bitcast, bf16[256,1152]{1,0:T(8,128)(2,1)S(1)} %get-tuple-element.66, f32[256]{0:T(256)S(1)} %add_rsqrt_fusion.1), kind=kOutput, calls=%fused_computation.60 | convolution fusion | flops 303267840 | bytes 2360328 | tf_op jit(solution)/shard_map/dot_general | solution.py:104
  109.7 3.2 %fusion.48 = f32[256,1152]{1,0:T(8,128)} fusion(bf16[256,1152]{1,0:T(8,128)(2,1)} %collective-permute-done.4, f32[]{:T(128)} %bitcast.34, f32[]{:T(128)} %bitcast, bf16[256,1152]{1,0:T(8,128)(2,1)S(1)} %get-tuple-element.60, f32[256]{0:T(256)S(1)} %add_rsqrt_fusion), kind=kOutput, calls=%fused_computation.59 | convolution fusion | flops 303267840 | bytes 2360328 | tf_op jit(solution)/shard_map/dot_general | solution.py:105
  112.9 3.6 %fusion.14 = (f32[256]{0:T(256)S(1)}, f32[256,1152]{1,0:T(8,128)}) fusion(bf16[256,1152]{1,0:T(8,128)(2,1)S(1)} %get-tuple-element.60, f32[256]{0:T(256)S(1)} %add_rsqrt_fusion, f32[256,1152]{1,0:T(8,128)} %fusion.48, f32[256,1152]{1,0:T(8,128)S(1)} %add.167, bf16[256,1152]{1,0:T(8,128)(2,1)} %collective-permute-done.3, f32[]{:T(128)} %bitcast.35, f32[]{:T(128)} %bitcast), kind=kOutput, calls=%fused_computation.20 | convolution fusion | flops 305331968 | bytes 4720648 | tf_op jit(solution)/shard_map/dot_general | solution.py:103
  116.5 3.7 %fusion.10 = (f32[256]{0:T(256)S(1)}, f32[256,1152]{1,0:T(8,128)}) fusion(bf16[256,1152]{1,0:T(8,128)(2,1)S(1)} %get-tuple-element.66, f32[256]{0:T(256)S(1)} %add_rsqrt_fusion.1, f32[256,1152]{1,0:T(8,128)} %fusion.49, f32[256,1152]{1,0:T(8,128)S(1)} %add.164, bf16[256,1152]{1,0:T(8,128)(2,1)} %collective-permute-done.2, f32[]{:T(128)} %bitcast.38, f32[]{:T(128)} %bitcast), kind=kOutput, calls=%fused_computation.16 | convolution fusion | flops 305331968 | bytes 4720648 | tf_op jit(solution)/shard_map/dot_general | solution.py:102
  120.2 3.2 %fusion.51 = (f32[256,1152]{1,0:T(8,128)}, f32[256,1152]{1,0:T(8,128)}) fusion(f32[256,1152]{1,0:T(8,128)S(1)} %copy-done, bf16[256,1152]{1,0:T(8,128)(2,1)S(1)} %get-tuple-element.60, f32[256,1152]{1,0:T(8,128)} %get-tuple-element.72, bf16[256,1152]{1,0:T(8,128)(2,1)S(1)} %get-tuple-element.66, f32[256]{0:T(256)S(1)} %get-tuple-element.69, ...), kind=kLoop, calls=%fused_computation.66 | loop fusion | flops 3538944 | bytes 5902337 | tf_op jit(solution)/shard_map/jit(_where)/select_n | solution.py:110
  (20 shorter events, 6.5 us)
Async XLA Ops:
  2.7 16.9 %collective-permute-start = (bf16[256,1152]{1,0:T(8,128)(2,1)S(1)}, bf16[256,1152]{1,0:T(8,128)(2,1)}, u32[]{:S(2)}, u32[]{:S(2)}) collective-permute-start(bf16[256,1152]{1,0:T(8,128)(2,1)S(1)} %fusion.6), channel_id=1, source_target_pairs={{0,8},{1,761},{2,10},{3,763},{4,12},{5,765},{6,14},{7,767},{8,16},... | collective-permute-start | bytes 1769480 | tf_op jit(solution)/shard_map/ppermute | solution.py:19
  6.3 17.9 %collective-permute-start.1 = (bf16[256,1152]{1,0:T(8,128)(2,1)S(1)}, bf16[256,1152]{1,0:T(8,128)(2,1)}, u32[]{:S(2)}, u32[]{:S(2)}) collective-permute-start(bf16[256,1152]{1,0:T(8,128)(2,1)S(1)} %fusion.9), channel_id=1, source_target_pairs={{0,760},{1,9},{2,762},{3,11},{4,764},{5,13},{6,766},{7,15},{8,0},{... | collective-permute-start | bytes 1769480 | tf_op jit(solution)/shard_map/ppermute | solution.py:19
  24.2 28.7 %collective-permute-start.2 = (bf16[256,1152]{1,0:T(8,128)(2,1)}, bf16[256,1152]{1,0:T(8,128)(2,1)}, u32[]{:S(2)}, u32[]{:S(2)}) collective-permute-start(bf16[256,1152]{1,0:T(8,128)(2,1)} %collective-permute-done), channel_id=1, source_target_pairs={{0,8},{1,761},{2,10},{3,763},{4,12},{5,765},{6,14},{7,767},{8,16},... | collective-permute-start | bytes 1769480 | tf_op jit(solution)/shard_map/ppermute | solution.py:19
  44.4 38.6 %collective-permute-start.3 = (bf16[256,1152]{1,0:T(8,128)(2,1)}, bf16[256,1152]{1,0:T(8,128)(2,1)}, u32[]{:S(2)}, u32[]{:S(2)}) collective-permute-start(bf16[256,1152]{1,0:T(8,128)(2,1)} %collective-permute-done.1), channel_id=1, source_target_pairs={{0,760},{1,9},{2,762},{3,11},{4,764},{5,13},{6,766},{7,15},{8,0},{... | collective-permute-start | bytes 1769480 | tf_op jit(solution)/shard_map/ppermute | solution.py:19
  57.9 24.3 %all-to-all-start = ((f32[64,1,128]{2,1,0:T(1,128)}), f32[64,1,128]{2,1,0:T(1,128)}, u32[]{:S(2)}, u32[]{:S(2)}) async-start(f32[64,1,128]{2,1,0:T(1,128)} %broadcast_in_dim.9), calls=%async_computation | async-start | bytes 65536 | tf_op jit(solution)/shard_map/all_to_all | solution.py:48
  73.8 31.5 %collective-permute-start.5 = (bf16[256,1152]{1,0:T(8,128)(2,1)}, bf16[256,1152]{1,0:T(8,128)(2,1)}, u32[]{:S(2)}, u32[]{:S(2)}) collective-permute-start(bf16[256,1152]{1,0:T(8,128)(2,1)} %collective-permute-done.2), channel_id=1, source_target_pairs={{0,8},{1,761},{2,10},{3,763},{4,12},{5,765},{6,14},{7,767},{8,16},... | collective-permute-start | bytes 1769480 | tf_op jit(solution)/shard_map/ppermute | solution.py:19
  83.0 22.3 %collective-permute-start.4 = (bf16[256,1152]{1,0:T(8,128)(2,1)}, bf16[256,1152]{1,0:T(8,128)(2,1)}, u32[]{:S(2)}, u32[]{:S(2)}) collective-permute-start(bf16[256,1152]{1,0:T(8,128)(2,1)} %collective-permute-done.3), channel_id=1, source_target_pairs={{0,760},{1,9},{2,762},{3,11},{4,764},{5,13},{6,766},{7,15},{8,0},{... | collective-permute-start | bytes 1769480 | tf_op jit(solution)/shard_map/ppermute | solution.py:19
  116.5 3.7 %copy-start = (f32[256,1152]{1,0:T(8,128)S(1)}, f32[256,1152]{1,0:T(8,128)}, u32[]{:S(2)}) copy-start(f32[256,1152]{1,0:T(8,128)} %get-tuple-element.70) | copy-start | bytes 3538948

commit v2 on v1

v2 whole, which is shorter than its diff:
```python
import functools

import jax
import jax.numpy as jnp
from jax import lax
from jax.experimental import pallas as pl
from jax.experimental.pallas import tpu as pltpu
from jax.sharding import Mesh, PartitionSpec as P

EPSILON = 1e-06
ROWS, D = 256, 1152
BLK_PARTS = (4, 3, 8)
GRP_PARTS = (4, 2)
N_BLK, N_GRP = 96, 8
AXES = ("x", "l", "y", "h", "c")
BF16, F32 = jnp.bfloat16, jnp.float32
PARAMS = pltpu.CompilerParams(vmem_limit_bytes=40 * 1024 * 1024)
CHUNK = 32

SMEM = pl.BlockSpec(memory_space=pltpu.SMEM)
VMEM = pl.BlockSpec(memory_space=pltpu.VMEM)
ANY = pl.BlockSpec(memory_space=pl.ANY)


def hop(value, steps):
    pairs = []
    for b in range(N_BLK):
        for g in range(N_GRP):
            way = steps if g % 2 == 0 else -steps
            pairs.append((b * N_GRP + g, ((b + way) % N_BLK) * N_GRP + g))
    return lax.ppermute(value, AXES, pairs)


def cosines(rows, cols):
    return lax.dot_general(rows, cols, (((1,), (1,)), ((), ())), preferred_element_type=F32)


def sigmoid_parts(x):
    small = jnp.exp(-jnp.abs(x))
    return small, jnp.where(x >= 0, 1.0, small) / (1.0 + small)


def folded(values):
    part = values[0:8]
    for r in range(8, ROWS, 8):
        part = part + values[r : r + 8]
    return part[:, 0:128] + part[:, 128:256]


def add_sums(sums_ref, cosine, logit, x, slope, small):
    softplus = jnp.maximum(x, 0.0) + jnp.log1p(small)
    sums_ref[0:8, :] += folded(softplus)
    sums_ref[8:16, :] += folded(slope * cosine)
    sums_ref[16:24, :] += folded(slope)


def logits(cosine, e_ref, b_ref):
    scale = jnp.exp(jnp.full((1, ROWS), e_ref[0], F32))
    return scale * cosine + b_ref[0]


def to_unit(source, out):
    for r in range(0, ROWS, CHUNK):
        v = source[r : r + CHUNK, :].astype(F32)
        inverse = lax.rsqrt(jnp.sum(v * v, axis=-1, keepdims=True) + EPSILON)
        out[r : r + CHUNK, :] = (v * inverse).astype(BF16)


def unit_kernel(image, text, p0, q0):
    even = lax.axis_index("c") == 0

    @pl.when(even)
    def _():
        to_unit(text, p0)
        to_unit(image, q0)

    @pl.when(jnp.logical_not(even))
    def _():
        to_unit(image, p0)
        to_unit(text, q0)


def units(image, text):
    rows = jax.ShapeDtypeStruct((ROWS, D), BF16)
    return pl.pallas_call(
        unit_kernel,
        out_shape=(rows, rows),
        in_specs=[VMEM, VMEM],
        out_specs=(VMEM, VMEM),
        compiler_params=PARAMS,
        cost_estimate=pl.CostEstimate(flops=2 * 10**6, bytes_accessed=2400000, transcendentals=512),
    )(image, text)


def own_kernel(e_ref, b_ref, p0, q0, d00, d00t, sums):
    i = lax.broadcasted_iota(jnp.int32, (ROWS, ROWS), 0)
    j = lax.broadcasted_iota(jnp.int32, (ROWS, ROWS), 1)
    pair = i == j
    sums[...] = jnp.zeros_like(sums)
    cosine = cosines(q0[...], p0[...])
    logit = logits(cosine, e_ref, b_ref)
    x = jnp.where(pair, -logit, logit)
    small, sig = sigmoid_parts(x)
    slope = jnp.where(pair, -sig, sig)
    add_sums(sums, cosine, logit, x, slope, small)
    d00[...] = slope.astype(BF16)
    logit = logits(cosines(p0[...], q0[...]), e_ref, b_ref)
    _, sig = sigmoid_parts(jnp.where(pair, -logit, logit))
    d00t[...] = jnp.where(pair, -sig, sig).astype(BF16)


def own(e, b, p0, q0):
    return pl.pallas_call(
        own_kernel,
        out_shape=(
            jax.ShapeDtypeStruct((ROWS, ROWS), BF16),
            jax.ShapeDtypeStruct((ROWS, ROWS), BF16),
            jax.ShapeDtypeStruct((24, 128), F32),
        ),
        in_specs=[SMEM, SMEM, VMEM, VMEM],
        out_specs=(VMEM, VMEM, VMEM),
        compiler_params=PARAMS,
        cost_estimate=pl.CostEstimate(flops=3 * 10**8, bytes_accessed=1500000, transcendentals=200000),
    )(e, b, p0, q0)


def middle_kernel(e_ref, b_ref, sums_in, p0, q0, p1, q1, d01, d10, sums):
    sums[...] = sums_in[...]
    cosine = cosines(q0[...], p1[...])
    logit = logits(cosine, e_ref, b_ref)
    small, slope = sigmoid_parts(logit)
    add_sums(sums, cosine, logit, logit, slope, small)
    d01[...] = slope.astype(BF16)
    cosine = cosines(q1[...], p1[...])
    logit = logits(cosine, e_ref, b_ref)
    small, slope = sigmoid_parts(logit)
    add_sums(sums, cosine, logit, logit, slope, small)
    _, slope = sigmoid_parts(logits(cosines(p0[...], q1[...]), e_ref, b_ref))
    d10[...] = slope.astype(BF16)


def middle(e, b, sums, p0, q0, p1, q1):
    return pl.pallas_call(
        middle_kernel,
        out_shape=(
            jax.ShapeDtypeStruct((ROWS, ROWS), BF16),
            jax.ShapeDtypeStruct((ROWS, ROWS), BF16),
            jax.ShapeDtypeStruct((24, 128), F32),
        ),
        in_specs=[SMEM, SMEM] + [VMEM] * 5,
        out_specs=(VMEM, VMEM, VMEM),
        compiler_params=PARAMS,
        cost_estimate=pl.CostEstimate(flops=5 * 10**8, bytes_accessed=2700000, transcendentals=300000),
    )(e, b, sums, p0, q0, p1, q1)


def last_kernel(e_ref, b_ref, sums_in, q1, p2, out, sums):
    sums[...] = sums_in[...]
    cosine = cosines(q1[...], p2[...])
    logit = logits(cosine, e_ref, b_ref)
    small, slope = sigmoid_parts(logit)
    add_sums(sums, cosine, logit, logit, slope, small)
    scale = jnp.exp(jnp.full((1, 1), e_ref[0], F32))
    loss = jnp.sum(sums[0:8, :], keepdims=True)
    by_scale = scale * jnp.sum(sums[8:16, :], keepdims=True)
    by_bias = jnp.sum(sums[16:24, :], keepdims=True)
    lane = lax.broadcasted_iota(jnp.int32, out.shape, 1)
    row = jnp.where(lane == 0, loss, jnp.where(lane == 1, by_scale, jnp.where(lane == 2, by_bias, 0.0)))
    out[...] = row


def last(e, b, sums, q1, p2, count):
    return pl.pallas_call(
        last_kernel,
        out_shape=jax.ShapeDtypeStruct((count, 128), F32),
        in_specs=[SMEM, SMEM] + [VMEM] * 3,
        out_specs=VMEM,
        scratch_shapes=[pltpu.VMEM((24, 128), F32)],
        compiler_params=PARAMS,
        cost_estimate=pl.CostEstimate(flops=2 * 10**8, bytes_accessed=1200000, transcendentals=100000),
    )(e, b, sums, q1, p2)


def block(k):
    return pl.ds(k * ROWS, ROWS)


def started(pairs, sems):
    copies = [pltpu.make_async_copy(src, dst, sems.at[n]) for n, (src, dst) in enumerate(pairs)]
    for copy in copies:
        copy.start()
    return copies


def either(chosen, first, second):
    @pl.when(chosen)
    def _():
        first.start()

    @pl.when(jnp.logical_not(chosen))
    def _():
        second.start()


def finish(e_ref, slopes, others, raw, out):
    scale = jnp.exp(jnp.full((1, 1), e_ref[0], F32))
    out[...] = jnp.dot(slopes[...], others[...], preferred_element_type=F32)
    for r in range(0, ROWS, CHUNK):
        rows = slice(r, r + CHUNK)
        v = raw[rows, :].astype(F32)
        inverse = lax.rsqrt(jnp.sum(v * v, axis=-1, keepdims=True) + EPSILON)
        u = v * inverse
        g = scale * out[rows, :]
        out[rows, :] = inverse * (g - u * jnp.sum(u * g, axis=-1, keepdims=True))


def slope_block(e_ref, b_ref, rows, cols):
    return sigmoid_parts(logits(cosines(rows, cols), e_ref, b_ref))[1].astype(BF16)


def q_kernel(early_call, e_ref, b_ref, image, text, p0, p1, p2, p3, q0, q2, d00, d01, *refs):
    out_image, out_text, d20, y, own, other, d, cross, raw, out, sems, out_sems = refs if early_call else refs[3:]
    early = jnp.logical_and(lax.axis_index("h") == 0, lax.axis_index("l") < 2)
    is_text = lax.axis_index("c") == 1
    mine = early if early_call else jnp.logical_not(early)

    @pl.when(mine)
    def _():
        copies = started(
            [
                (q0, own),
                (p2, y.at[block(2), :]),
                (p3, y.at[block(3), :]),
                (p0, y.at[block(0), :]),
                (q2, other),
                (p1, y.at[block(1), :]),
                (d00, d.at[:, block(0)]),
                (d01, d.at[:, block(1)]),
            ],
            sems,
        )
        from_text = pltpu.make_async_copy(text, raw, sems.at[8])
        from_image = pltpu.make_async_copy(image, raw, sems.at[8])
        either(is_text, from_text, from_image)
        copies[0].wait()
        for k in (2, 3):
            copies[k - 1].wait()
            d[:, block(k)] = slope_block(e_ref, b_ref, own[...], y[block(k), :])
        copies[3].wait()
        copies[4].wait()
        cross[...] = slope_block(e_ref, b_ref, y[block(0), :], other[...])
        cross_copy = pltpu.make_async_copy(cross, d20, out_sems.at[0])
        cross_copy.start()
        for copy in copies[5:]:
            copy.wait()
        from_text.wait()
        finish(e_ref, d, y, raw, out)
        to_text = pltpu.make_async_copy(out, out_text, out_sems.at[1])
        either(is_text, to_text, pltpu.make_async_copy(out, out_image, out_sems.at[1]))
        cross_copy.wait()
        to_text.wait()


def p_kernel(e_ref, b_ref, image, text, q0, q1, q2, q3, p0, d00t, d10, d20, *refs):
    _, _, out_image, out_text, y, own, d, raw, out, sems, out_sem = refs
    is_text = lax.axis_index("c") == 0
    copies = started(
        [
            (p0, own),
            (q3, y.at[block(3), :]),
            (q0, y.at[block(0), :]),
            (q1, y.at[block(1), :]),
            (q2, y.at[block(2), :]),
            (d00t, d.at[:, block(0)]),
            (d10, d.at[:, block(1)]),
            (d20, d.at[:, block(2)]),
        ],
        sems,
    )
    from_text = pltpu.make_async_copy(text, raw, sems.at[8])
    from_image = pltpu.make_async_copy(image, raw, sems.at[8])
    either(is_text, from_text, from_image)
    copies[0].wait()
    copies[1].wait()
    d[:, block(3)] = slope_block(e_ref, b_ref, own[...], y[block(3), :])
    for copy in copies[2:]:
        copy.wait()
    from_text.wait()
    finish(e_ref, d, y, raw, out)
    to_text = pltpu.make_async_copy(out, out_text, out_sem)
    either(is_text, to_text, pltpu.make_async_copy(out, out_image, out_sem))
    to_text.wait()


GRAD = jax.ShapeDtypeStruct((ROWS, D), F32)
SLOPES = jax.ShapeDtypeStruct((ROWS, ROWS), BF16)


def q_side(args, previous):
    early_call = previous is None
    n = len(args)
    return pl.pallas_call(
        functools.partial(q_kernel, early_call),
        out_shape=(GRAD, GRAD, SLOPES),
        in_specs=[SMEM, SMEM] + [ANY] * (n - 2 + (0 if early_call else 3)),
        out_specs=(ANY, ANY, ANY),
        input_output_aliases={} if early_call else {n: 0, n + 1: 1, n + 2: 2},
        scratch_shapes=[
            pltpu.VMEM((4 * ROWS, D), BF16),
            pltpu.VMEM((ROWS, D), BF16),
            pltpu.VMEM((ROWS, D), BF16),
            pltpu.VMEM((ROWS, 4 * ROWS), BF16),
            pltpu.VMEM((ROWS, ROWS), BF16),
            pltpu.VMEM((ROWS, D), BF16),
            pltpu.VMEM((ROWS, D), F32),
            pltpu.SemaphoreType.DMA((9,)),
            pltpu.SemaphoreType.DMA((2,)),
        ],
        compiler_params=PARAMS,
        cost_estimate=pl.CostEstimate(flops=10**9, bytes_accessed=5000000, transcendentals=200000),
    )(*args, *([] if early_call else previous))


def p_side(args, previous):
    n = len(args)
    return pl.pallas_call(
        p_kernel,
        out_shape=(GRAD, GRAD),
        in_specs=[SMEM, SMEM] + [ANY] * n,
        out_specs=(ANY, ANY),
        input_output_aliases={n: 0, n + 1: 1},
        scratch_shapes=[
            pltpu.VMEM((4 * ROWS, D), BF16),
            pltpu.VMEM((ROWS, D), BF16),
            pltpu.VMEM((ROWS, 4 * ROWS), BF16),
            pltpu.VMEM((ROWS, D), BF16),
            pltpu.VMEM((ROWS, D), F32),
            pltpu.SemaphoreType.DMA((9,)),
            pltpu.SemaphoreType.DMA,
        ],
        compiler_params=PARAMS,
        cost_estimate=pl.CostEstimate(flops=10**9, bytes_accessed=5000000, transcendentals=200000),
    )(*args, *previous)


def body(image, text, e, b):
    bar = lax.optimization_barrier
    p0, q0 = units(image, text)
    p1 = hop(p0, 1)
    q1 = hop(q0, -1)
    d00, d00t, sums = own(e, b, p0, q0)
    sums, p1, q1 = bar((sums, p1, q1))

    p2 = hop(p1, 1)
    d01, d10, sums = middle(e, b, sums, p0, q0, p1, q1)
    sums, q1s = bar((sums, q1))
    q2 = hop(q1s, -1)
    row = last(e, b, sums, q1, p2, 64)
    row, p2s = bar((row, p2))
    p3 = hop(p2s, 1)
    row = lax.all_to_all(row, ("x", "y", "c"), 0, 0, tiled=True)
    row, q2s = bar((row, q2))
    q3 = hop(q2s, -1)
    row = jnp.sum(row, axis=0, keepdims=True)
    q_args = (e, b, image, text, p0, p1, p2, p3, q0, q2s, d00, d01)
    row, done = bar((row, q_side(q_args, None)))
    row = lax.all_to_all(jnp.broadcast_to(row, (12, 128)), ("l", "h"), 0, 0, tiled=True)
    row, done = bar((row, done))
    totals = jnp.sum(row, axis=0)[:3] / jnp.float32(ROWS * N_BLK * N_GRP)
    grad_image, grad_text, d20 = q_side(q_args, done)
    p_args = (e, b, image, text, q0, q1, q2s, q3, p0, d00t, d10, d20)
    grad_image, grad_text = p_side(p_args, (grad_image, grad_text))
    return grad_image, grad_text, totals


def solution(mesh):
    fine = Mesh(mesh.devices.reshape(BLK_PARTS + GRP_PARTS), AXES)
    split = P(AXES, None)
    return jax.shard_map(
        body,
        mesh=fine,
        in_specs=(split, split, P(), P()),
        out_specs=(split, split, P()),
        check_vma=False,
    )
```

time: 124 us -> 113 us (0.911)
  the two profiles are of different devices: /device:TPU:2 before, /device:TPU:128 now
where the time goes in v2:
time: 113 us; the launch traced here: 112 us
  starting transfers between devices  45.5 us (40%)
  waiting for transfers between devices  19.7 us (17%)
  blocking collectives  18.9 us (17%)
  Pallas kernels  13.5 us (12%)
  local copies, waits for them, and re-layouts  11.3 us (10%)
  between operations  2.15 us (2%)
  other arithmetic  1.32 us (1%)
    all_to_all x1, starting transfers between devices, body(): row = lax.all_to_all(row, ('x', 'y', 'c'), 0, 0, tiled=True)  25.3 us
    ppermute x6, starting transfers between devices, hop(): return lax.ppermute(value, AXES, pairs)  20.2 us
    all_to_all x1, blocking collectives, body(): lax.all_to_all(jnp.broadcast_to(row, (12, 128)), ('l', 'h'), 0, 0, tiled=...  18.9 us
    unnamed x41, local copies, waits for them, and re-layouts  11.3 us
    ppermute x6, waiting for transfers between devices, hop(): return lax.ppermute(value, AXES, pairs)  10.5 us
    all_to_all x1, waiting for transfers between devices, body(): row = lax.all_to_all(row, ('x', 'y', 'c'), 0, 0, tiled=True)  9.26 us
    pallas_call x2, Pallas kernels, q_side(): pl.pallas_call(functools.partial(q_kernel, early_call), out_shape=(GRAD,...  5.39 us
    pallas_call x1, Pallas kernels, p_side(): pl.pallas_call(p_kernel, out_shape=(GRAD, GRAD), in_specs=[SMEM, SMEM] +...  4.1 us
  transfers between devices with their start and end apart: 7, of which 3 were waited for; matrix products, arithmetic and copies ran while one was open for 1% of the time, Pallas kernels for 8%

profile of v2, /device:TPU:128, one launch (start us, length us, event | category | flops | bytes accessed | tf_op | source)
XLA Modules:
  0.0 112.5 jit_solution(1346951398058910151)
XLA Ops:
  0.6 1.1 copy-done
  1.7 1.1 copy-done.2
  3.1 3.5 %collective-permute-start = (bf16[256,1152]{1,0:T(8,128)(2,1)S(1)}, bf16[256,1152]{1,0:T(8,128)(2,1)S(1)}, u32[]{:S(2)}, u32[]{:S(2)}) collective-permute-start(bf16[256,1152]{1,0:T(8,128)(2,1)S(1)} %get-tuple-element.37.p0), channel_id=1, source_target_pairs={{0,8},{1,761},{2,10},{3,763},{4,12},{5,765},{6,14},{7,767},{8,16},... | collective-permute-start | bytes 1769480 | tf_op jit(solution)/shard_map/ppermute | solution.py:31
  6.6 4.5 %collective-permute-start.1 = (bf16[256,1152]{1,0:T(8,128)(2,1)S(1)}, bf16[256,1152]{1,0:T(8,128)(2,1)S(1)}, u32[]{:S(2)}, u32[]{:S(2)}) collective-permute-start(bf16[256,1152]{1,0:T(8,128)(2,1)S(1)} %get-tuple-element.36.q0), channel_id=1, source_target_pairs={{0,760},{1,9},{2,762},{3,11},{4,764},{5,13},{6,766},{7,15},{8,0},{... | collective-permute-start | bytes 1769480 | tf_op jit(solution)/shard_map/ppermute | solution.py:31
  13.3 7.0 %collective-permute-done.p1 = bf16[256,1152]{1,0:T(8,128)(2,1)S(1)} collective-permute-done((bf16[256,1152]{1,0:T(8,128)(2,1)S(1)}, bf16[256,1152]{1,0:T(8,128)(2,1)S(1)}, u32[]{:S(2)}, u32[]{:S(2)}) %collective-permute-start) | collective-permute-done | bytes 589856 | tf_op jit(solution)/shard_map/ppermute | solution.py:31
  20.2 3.3 %collective-permute-start.2 = (bf16[256,1152]{1,0:T(8,128)(2,1)S(1)}, bf16[256,1152]{1,0:T(8,128)(2,1)}, u32[]{:S(2)}, u32[]{:S(2)}) collective-permute-start(bf16[256,1152]{1,0:T(8,128)(2,1)S(1)} %collective-permute-done.p1), channel_id=1, source_target_pairs={{0,8},{1,761},{2,10},{3,763},{4,12},{5,765},{6,14},{7,767},{8,16},... | collective-permute-start | bytes 1769480 | tf_op jit(solution)/shard_map/ppermute | solution.py:31
  23.6 1.1 shard_map.69
  26.0 5.1 %collective-permute-start.3 = (bf16[256,1152]{1,0:T(8,128)(2,1)S(1)}, bf16[256,1152]{1,0:T(8,128)(2,1)S(1)}, u32[]{:S(2)}, u32[]{:S(2)}) collective-permute-start(bf16[256,1152]{1,0:T(8,128)(2,1)S(1)} %collective-permute-done.1.q1), channel_id=1, source_target_pairs={{0,760},{1,9},{2,762},{3,11},{4,764},{5,13},{6,766},{7,15},{8,0},{... | collective-permute-start | bytes 1769480 | tf_op jit(solution)/shard_map/ppermute | solution.py:31
  31.1 3.5 %collective-permute-done.2.p2 = bf16[256,1152]{1,0:T(8,128)(2,1)} collective-permute-done((bf16[256,1152]{1,0:T(8,128)(2,1)S(1)}, bf16[256,1152]{1,0:T(8,128)(2,1)}, u32[]{:S(2)}, u32[]{:S(2)}) %collective-permute-start.2) | collective-permute-done | bytes 589856 | tf_op jit(solution)/shard_map/ppermute | solution.py:31
  34.6 1.7 %shard_map.70 = f32[64,128]{1,0:T(8,128)S(1)} custom-call(f32[1]{0:T(128)S(6)} %copy.21.e_ref, f32[1]{0:T(128)S(6)} %copy.22.b_ref, f32[24,128]{1,0:T(8,128)S(1)} %get-tuple-element.43.sums_in, bf16[256,1152]{1,0:T(8,128)(2,1)S(1)} %collective-permute-done.1.q1, bf16[256,1152]{1,0:T(8,128)(2,1)} %collective-permute-done.2.p2), custom_call_target="tpu_custom_call" | custom-call | flops 200000000 | bytes 1200000 | tf_op jit(solution)/shard_map/pallas_call | solution.py:173
  37.0 1.9 %collective-permute-start.5 = (bf16[256,1152]{1,0:T(8,128)(2,1)}, bf16[256,1152]{1,0:T(8,128)(2,1)}, u32[]{:S(2)}, u32[]{:S(2)}) collective-permute-start(bf16[256,1152]{1,0:T(8,128)(2,1)} %collective-permute-done.2.p2), channel_id=1, source_target_pairs={{0,8},{1,761},{2,10},{3,763},{4,12},{5,765},{6,14},{7,767},{8,16},... | collective-permute-start | bytes 1769480 | tf_op jit(solution)/shard_map/ppermute | solution.py:31
  38.9 25.3 %all-to-all-start = ((f32[64,1,128]{2,1,0:T(1,128)}), f32[64,1,128]{2,1,0:T(1,128)}, u32[]{:S(2)}, u32[]{:S(2)}) async-start(f32[64,1,128]{2,1,0:T(1,128)} %bitcast.9), calls=%async_computation | async-start | bytes 65536 | tf_op jit(solution)/shard_map/all_to_all | solution.py:361
  64.2 9.3 %all-to-all-done = f32[64,1,128]{2,1,0:T(1,128)} async-done(((f32[64,1,128]{2,1,0:T(1,128)}), f32[64,1,128]{2,1,0:T(1,128)}, u32[]{:S(2)}, u32[]{:S(2)}) %all-to-all-start) | async-done | bytes 32800 | tf_op jit(solution)/shard_map/all_to_all | solution.py:361
  73.5 1.9 %collective-permute-start.4 = (bf16[256,1152]{1,0:T(8,128)(2,1)S(1)}, bf16[256,1152]{1,0:T(8,128)(2,1)}, u32[]{:S(2)}, u32[]{:S(2)}) collective-permute-start(bf16[256,1152]{1,0:T(8,128)(2,1)S(1)} %collective-permute-done.3.q2), channel_id=1, source_target_pairs={{0,760},{1,9},{2,762},{3,11},{4,764},{5,13},{6,766},{7,15},{8,0},{... | collective-permute-start | bytes 1769480 | tf_op jit(solution)/shard_map/ppermute | solution.py:31
  76.2 1.1 copy-done.5
  77.3 0.9 copy-done.8
  78.2 0.9 copy-done.11
  79.8 18.9 %all_to_all.21 = f32[12,1,128]{2,1,0:T(1,128)S(1)} all-to-all(f32[12,1,128]{2,1,0:T(1,128)S(1)} %broadcast_in_dim.9), channel_id=1, replica_groups=mesh['x'=4,'l'=3,'y'=8,'h'=4,'c'=2] {'l','h'}, dimensions={0} | all-to-all | bytes 12288 | tf_op jit(solution)/shard_map/all_to_all | solution.py:367
  98.8 1.1 copy-done.6
  99.9 0.9 copy-done.9
  100.8 0.9 copy-done.12
  101.7 0.9 copy-done.14
  102.6 5.3 %shard_map.72 = (f32[256,1152]{1,0:T(8,128)}, f32[256,1152]{1,0:T(8,128)}, bf16[256,256]{1,0:T(8,128)(2,1)S(1)}) custom-call(f32[1]{0:T(128)S(6)} %copy.21.e_ref, f32[1]{0:T(128)S(6)} %copy.22.b_ref, bf16[256,1152]{1,0:T(8,128)(2,1)S(1)} %copy-done.1, bf16[256,1152]{1,0:T(8,128)(2,1)S(1)} %copy-done.3, ...), custom_call_target="tpu_custom_call", output_to_operand_aliasing={{0}: (12, {}), {1}: (13, {}), {2}: (14, {})} | custom-call | flops 1000000000 | bytes 5000000 | tf_op jit(solution)/shard_map/pallas_call | solution.py:302
  108.4 4.1 %shard_map.73 = (f32[256,1152]{1,0:T(8,128)}, f32[256,1152]{1,0:T(8,128)}) custom-call(f32[1]{0:T(128)S(6)} %copy.21.e_ref, f32[1]{0:T(128)S(6)} %copy.22.b_ref, bf16[256,1152]{1,0:T(8,128)(2,1)S(1)} %copy-done.1, bf16[256,1152]{1,0:T(8,128)(2,1)S(1)} %copy-done.3, ...), custom_call_target="tpu_custom_call", output_to_operand_aliasing={{0}: (12, {}), {1}: (13, {})} | custom-call | flops 1000000000 | bytes 5000000 | tf_op jit(solution)/shard_map/pallas_call | solution.py:326
  (43 shorter events, 5.2 us)
Async XLA Ops:
  0.6 1.1 copy-start
  1.7 1.1 copy-start.2
  3.1 17.1 %collective-permute-start = (bf16[256,1152]{1,0:T(8,128)(2,1)S(1)}, bf16[256,1152]{1,0:T(8,128)(2,1)S(1)}, u32[]{:S(2)}, u32[]{:S(2)}) collective-permute-start(bf16[256,1152]{1,0:T(8,128)(2,1)S(1)} %get-tuple-element.37.p0), channel_id=1, source_target_pairs={{0,8},{1,761},{2,10},{3,763},{4,12},{5,765},{6,14},{7,767},{8,16},... | collective-permute-start | bytes 1769480 | tf_op jit(solution)/shard_map/ppermute | solution.py:31
  6.6 13.6 %collective-permute-start.1 = (bf16[256,1152]{1,0:T(8,128)(2,1)S(1)}, bf16[256,1152]{1,0:T(8,128)(2,1)S(1)}, u32[]{:S(2)}, u32[]{:S(2)}) collective-permute-start(bf16[256,1152]{1,0:T(8,128)(2,1)S(1)} %get-tuple-element.36.q0), channel_id=1, source_target_pairs={{0,760},{1,9},{2,762},{3,11},{4,764},{5,13},{6,766},{7,15},{8,0},{... | collective-permute-start | bytes 1769480 | tf_op jit(solution)/shard_map/ppermute | solution.py:31
  13.2 11.4 %copy-start.7 = (bf16[256,256]{1,0:T(8,128)(2,1)}, bf16[256,256]{1,0:T(8,128)(2,1)S(1)}, u32[]{:S(2)}) copy-start(bf16[256,256]{1,0:T(8,128)(2,1)S(1)} %get-tuple-element.50.d00) | copy-start | bytes 393220
  13.2 11.4 %copy-start.15 = (bf16[256,256]{1,0:T(8,128)(2,1)}, bf16[256,256]{1,0:T(8,128)(2,1)S(1)}, u32[]{:S(2)}) copy-start(bf16[256,256]{1,0:T(8,128)(2,1)S(1)} %get-tuple-element.47.d00t) | copy-start | bytes 393220
  20.2 4.4 %copy-start.4 = (bf16[256,1152]{1,0:T(8,128)(2,1)}, bf16[256,1152]{1,0:T(8,128)(2,1)S(1)}, u32[]{:S(2)}) copy-start(bf16[256,1152]{1,0:T(8,128)(2,1)S(1)} %collective-permute-done.p1) | copy-start | bytes 1769476
  20.2 14.4 %collective-permute-start.2 = (bf16[256,1152]{1,0:T(8,128)(2,1)S(1)}, bf16[256,1152]{1,0:T(8,128)(2,1)}, u32[]{:S(2)}, u32[]{:S(2)}) collective-permute-start(bf16[256,1152]{1,0:T(8,128)(2,1)S(1)} %collective-permute-done.p1), channel_id=1, source_target_pairs={{0,8},{1,761},{2,10},{3,763},{4,12},{5,765},{6,14},{7,767},{8,16},... | collective-permute-start | bytes 1769480 | tf_op jit(solution)/shard_map/ppermute | solution.py:31
  24.7 0.7 copy-start.10
  26.0 50.2 %copy-start.1 = (bf16[256,1152]{1,0:T(8,128)(2,1)S(1)}, bf16[256,1152]{1,0:T(8,128)(2,1)}, u32[]{:S(2)}) copy-start(bf16[256,1152]{1,0:T(8,128)(2,1)} %image.7) | copy-start | bytes 1769476
  26.0 50.2 %copy-start.3 = (bf16[256,1152]{1,0:T(8,128)(2,1)S(1)}, bf16[256,1152]{1,0:T(8,128)(2,1)}, u32[]{:S(2)}) copy-start(bf16[256,1152]{1,0:T(8,128)(2,1)} %text.7) | copy-start | bytes 1769476
  26.0 38.2 %collective-permute-start.3 = (bf16[256,1152]{1,0:T(8,128)(2,1)S(1)}, bf16[256,1152]{1,0:T(8,128)(2,1)S(1)}, u32[]{:S(2)}, u32[]{:S(2)}) collective-permute-start(bf16[256,1152]{1,0:T(8,128)(2,1)S(1)} %collective-permute-done.1.q1), channel_id=1, source_target_pairs={{0,760},{1,9},{2,762},{3,11},{4,764},{5,13},{6,766},{7,15},{8,0},{... | collective-permute-start | bytes 1769480 | tf_op jit(solution)/shard_map/ppermute | solution.py:31
  37.0 39.2 %collective-permute-start.5 = (bf16[256,1152]{1,0:T(8,128)(2,1)}, bf16[256,1152]{1,0:T(8,128)(2,1)}, u32[]{:S(2)}, u32[]{:S(2)}) collective-permute-start(bf16[256,1152]{1,0:T(8,128)(2,1)} %collective-permute-done.2.p2), channel_id=1, source_target_pairs={{0,8},{1,761},{2,10},{3,763},{4,12},{5,765},{6,14},{7,767},{8,16},... | collective-permute-start | bytes 1769480 | tf_op jit(solution)/shard_map/ppermute | solution.py:31
  38.9 34.6 %all-to-all-start = ((f32[64,1,128]{2,1,0:T(1,128)}), f32[64,1,128]{2,1,0:T(1,128)}, u32[]{:S(2)}, u32[]{:S(2)}) async-start(f32[64,1,128]{2,1,0:T(1,128)} %bitcast.9), calls=%async_computation | async-start | bytes 65536 | tf_op jit(solution)/shard_map/all_to_all | solution.py:361
  73.5 34.9 %collective-permute-start.4 = (bf16[256,1152]{1,0:T(8,128)(2,1)S(1)}, bf16[256,1152]{1,0:T(8,128)(2,1)}, u32[]{:S(2)}, u32[]{:S(2)}) collective-permute-start(bf16[256,1152]{1,0:T(8,128)(2,1)S(1)} %collective-permute-done.3.q2), channel_id=1, source_target_pairs={{0,760},{1,9},{2,762},{3,11},{4,764},{5,13},{6,766},{7,15},{8,0},{... | collective-permute-start | bytes 1769480 | tf_op jit(solution)/shard_map/ppermute | solution.py:31
  76.2 1.1 copy-start.5
  77.3 0.9 copy-start.8
  78.2 0.9 copy-start.11
  98.8 1.1 copy-start.6
  99.9 0.9 copy-start.9
  100.8 0.9 copy-start.12
  101.7 0.9 copy-start.14
  102.6 5.8 %copy-start.16 = (bf16[256,256]{1,0:T(8,128)(2,1)S(1)}, bf16[256,256]{1,0:T(8,128)(2,1)}, u32[]{:S(2)}) copy-start(bf16[256,256]{1,0:T(8,128)(2,1)} %copy-done.15) | copy-start | bytes 393220
  102.6 5.8 %copy-start.18 = (bf16[256,256]{1,0:T(8,128)(2,1)S(1)}, bf16[256,256]{1,0:T(8,128)(2,1)}, u32[]{:S(2)}) copy-start(bf16[256,256]{1,0:T(8,128)(2,1)} %copy-done.17) | copy-start | bytes 393220
  (3 other events, 1.9 us)

commit v3 on v2

--- a/solution.py
+++ b/solution.py
@@ -14,12 +14,14 @@
 N_BLK, N_GRP = 96, 8
 AXES = ("x", "l", "y", "h", "c")
 BF16, F32 = jnp.bfloat16, jnp.float32
-PARAMS = pltpu.CompilerParams(vmem_limit_bytes=40 * 1024 * 1024)
+PARAMS = pltpu.CompilerParams(vmem_limit_bytes=16 * 1024 * 1024)
+WHOLE = pltpu.CompilerParams(vmem_limit_bytes=60 * 1024 * 1024)
 CHUNK = 32
+EARLY_PLANES = 5
 
 SMEM = pl.BlockSpec(memory_space=pltpu.SMEM)
 VMEM = pl.BlockSpec(memory_space=pltpu.VMEM)
-ANY = pl.BlockSpec(memory_space=pl.ANY)
+HBM = pl.BlockSpec(memory_space=pltpu.HBM)
 
 
 def hop(value, steps):
@@ -59,25 +61,41 @@
     return scale * cosine + b_ref[0]
 
 
-def to_unit(source, out):
-    for r in range(0, ROWS, CHUNK):
-        v = source[r : r + CHUNK, :].astype(F32)
-        inverse = lax.rsqrt(jnp.sum(v * v, axis=-1, keepdims=True) + EPSILON)
-        out[r : r + CHUNK, :] = (v * inverse).astype(BF16)
-
-
-def unit_kernel(image, text, p0, q0):
+PART = 64
+
+
+def unit_kernel(image, text, p0, q0, raw, sems):
     even = lax.axis_index("c") == 0
+    loads = {}
+    for name, source in (("image", image), ("text", text)):
+        for side in range(2):
+            for n in range(ROWS // PART):
+                rows = pl.ds(n * PART, PART)
+                loads[name, side, n] = pltpu.make_async_copy(
+                    source.at[rows, :], raw.at[side, rows, :], sems.at[side, n]
+                )
 
     @pl.when(even)
     def _():
-        to_unit(text, p0)
-        to_unit(image, q0)
+        for n in range(ROWS // PART):
+            loads["text", 0, n].start()
+        for n in range(ROWS // PART):
+            loads["image", 1, n].start()
 
     @pl.when(jnp.logical_not(even))
     def _():
-        to_unit(image, p0)
-        to_unit(text, q0)
+        for n in range(ROWS // PART):
+            loads["image", 0, n].start()
+        for n in range(ROWS // PART):
+            loads["text", 1, n].start()
+
+    for side, out in enumerate((p0, q0)):
+        for n in range(ROWS // PART):
+            loads["image", side, n].wait()
+            for r in range(n * PART, (n + 1) * PART, CHUNK):
+                v = raw[side, r : r + CHUNK, :].astype(F32)
+                inverse = lax.rsqrt(jnp.sum(v * v, axis=-1, keepdims=True) + EPSILON)
+                out[r : r + CHUNK, :] = (v * inverse).astype(BF16)
 
 
 def units(image, text):
@@ -85,9 +103,10 @@
     return pl.pallas_call(
         unit_kernel,
         out_shape=(rows, rows),
-        in_specs=[VMEM, VMEM],
+        in_specs=[HBM, HBM],
         out_specs=(VMEM, VMEM),
-        compiler_params=PARAMS,
+        scratch_shapes=[pltpu.VMEM((2, ROWS, D), BF16), pltpu.SemaphoreType.DMA((2, ROWS // PART))],
+        compiler_params=WHOLE,
         cost_estimate=pl.CostEstimate(flops=2 * 10**6, bytes_accessed=2400000, transcendentals=512),
     )(image, text)
 
@@ -202,7 +221,7 @@
         second.start()
 
 
-def finish(e_ref, slopes, others, raw, out):
+def finish(e_ref, slopes, others, raw, out, is_text, out_image, out_text, sem):
     scale = jnp.exp(jnp.full((1, 1), e_ref[0], F32))
     out[...] = jnp.dot(slopes[...], others[...], preferred_element_type=F32)
     for r in range(0, ROWS, CHUNK):
@@ -212,6 +231,14 @@
         u = v * inverse
         g = scale * out[rows, :]
         out[rows, :] = inverse * (g - u * jnp.sum(u * g, axis=-1, keepdims=True))
+        if (r + CHUNK) % PART == 0:
+            part = pl.ds(r + CHUNK - PART, PART)
+            either(
+                is_text,
+                pltpu.make_async_copy(out.at[part, :], out_text.at[part, :], sem),
+                pltpu.make_async_copy(out.at[part, :], out_image.at[part, :], sem),
+            )
+    pltpu.make_async_copy(out, out_text, sem).wait()
 
 
 def slope_block(e_ref, b_ref, rows, cols):
@@ -220,7 +247,7 @@
 
 def q_kernel(early_call, e_ref, b_ref, image, text, p0, p1, p2, p3, q0, q2, d00, d01, *refs):
     out_image, out_text, d20, y, own, other, d, cross, raw, out, sems, out_sems = refs if early_call else refs[3:]
-    early = jnp.logical_and(lax.axis_index("h") == 0, lax.axis_index("l") < 2)
+    early = 3 * lax.axis_index("h") + lax.axis_index("l") < EARLY_PLANES
     is_text = lax.axis_index("c") == 1
     mine = early if early_call else jnp.logical_not(early)
 
@@ -254,11 +281,8 @@
         for copy in copies[5:]:
             copy.wait()
         from_text.wait()
-        finish(e_ref, d, y, raw, out)
-        to_text = pltpu.make_async_copy(out, out_text, out_sems.at[1])
-        either(is_text, to_text, pltpu.make_async_copy(out, out_image, out_sems.at[1]))
+        finish(e_ref, d, y, raw, out, is_text, out_image, out_text, out_sems.at[1])
         cross_copy.wait()
-        to_text.wait()
 
 
 def p_kernel(e_ref, b_ref, image, text, q0, q1, q2, q3, p0, d00t, d10, d20, *refs):
@@ -286,10 +310,7 @@
     for copy in copies[2:]:
         copy.wait()
     from_text.wait()
-    finish(e_ref, d, y, raw, out)
-    to_text = pltpu.make_async_copy(out, out_text, out_sem)
-    either(is_text, to_text, pltpu.make_async_copy(out, out_image, out_sem))
-    to_text.wait()
+    finish(e_ref, d, y, raw, out, is_text, out_image, out_text, out_sem)
 
 
 GRAD = jax.ShapeDtypeStruct((ROWS, D), F32)
@@ -302,8 +323,8 @@
     return pl.pallas_call(
         functools.partial(q_kernel, early_call),
         out_shape=(GRAD, GRAD, SLOPES),
-        in_specs=[SMEM, SMEM] + [ANY] * (n - 2 + (0 if early_call else 3)),
-        out_specs=(ANY, ANY, ANY),
+        in_specs=[SMEM, SMEM] + [HBM] * (n - 2 + (0 if early_call else 3)),
+        out_specs=(HBM, HBM, HBM),
         input_output_aliases={} if early_call else {n: 0, n + 1: 1, n + 2: 2},
         scratch_shapes=[
             pltpu.VMEM((4 * ROWS, D), BF16),
@@ -316,7 +337,7 @@
             pltpu.SemaphoreType.DMA((9,)),
             pltpu.SemaphoreType.DMA((2,)),
         ],
-        compiler_params=PARAMS,
+        compiler_params=WHOLE,
         cost_estimate=pl.CostEstimate(flops=10**9, bytes_accessed=5000000, transcendentals=200000),
     )(*args, *([] if early_call else previous))
 
@@ -326,8 +347,8 @@
     return pl.pallas_call(
         p_kernel,
         out_shape=(GRAD, GRAD),
-        in_specs=[SMEM, SMEM] + [ANY] * n,
-        out_specs=(ANY, ANY),
+        in_specs=[SMEM, SMEM] + [HBM] * n,
+        out_specs=(HBM, HBM),
         input_output_aliases={n: 0, n + 1: 1},
         scratch_shapes=[
             pltpu.VMEM((4 * ROWS, D), BF16),
@@ -338,7 +359,7 @@
             pltpu.SemaphoreType.DMA((9,)),
             pltpu.SemaphoreType.DMA,
         ],
-        compiler_params=PARAMS,
+        compiler_params=WHOLE,
         cost_estimate=pl.CostEstimate(flops=10**9, bytes_accessed=5000000, transcendentals=200000),
     )(*args, *previous)
 
@@ -347,16 +368,14 @@
     bar = lax.optimization_barrier
     p0, q0 = units(image, text)
     p1 = hop(p0, 1)
-    q1 = hop(q0, -1)
     d00, d00t, sums = own(e, b, p0, q0)
-    sums, p1, q1 = bar((sums, p1, q1))
-
+    q0s, sums = bar((q0, sums))
+    q1 = hop(q0s, -1)
     p2 = hop(p1, 1)
     d01, d10, sums = middle(e, b, sums, p0, q0, p1, q1)
-    sums, q1s = bar((sums, q1))
+    row = last(e, b, sums, q1, p2, 64)
+    row, q1s, p2s = bar((row, q1, p2))
     q2 = hop(q1s, -1)
-    row = last(e, b, sums, q1, p2, 64)
-    row, p2s = bar((row, p2))
     p3 = hop(p2s, 1)
     row = lax.all_to_all(row, ("x", "y", "c"), 0, 0, tiled=True)
     row, q2s = bar((row, q2))

time: 113 us -> 102 us (0.903)
  the two profiles are of different devices: /device:TPU:128 before, /device:TPU:2 now
where the time goes in v3:
time: 102 us
  blocking collectives  38.5 us (38%)
  starting transfers between devices  24.9 us (24%)
  waiting for transfers between devices  15 us (15%)
  Pallas kernels  14.9 us (15%)
  local copies, waits for them, and re-layouts  5.72 us (6%)
  between operations  2.11 us (2%)
    all_to_all x1, blocking collectives, body(): row = lax.all_to_all(row, ('x', 'y', 'c'), 0, 0, tiled=True)  26 us
    ppermute x6, starting transfers between devices, hop(): return lax.ppermute(value, AXES, pairs)  24.9 us
    ppermute x6, waiting for transfers between devices, hop(): return lax.ppermute(value, AXES, pairs)  15 us
    all_to_all x1, blocking collectives, body(): lax.all_to_all(jnp.broadcast_to(row, (12, 128)), ('l', 'h'), 0, 0, tiled=...  12.5 us
    unnamed x25, local copies, waits for them, and re-layouts  5.71 us
    pallas_call x2, Pallas kernels, q_side(): pl.pallas_call(functools.partial(q_kernel, early_call), out_shape=(GRAD,...  5.17 us
    pallas_call x1, Pallas kernels, p_side(): pl.pallas_call(p_kernel, out_shape=(GRAD, GRAD), in_specs=[SMEM, SMEM] +...  4.29 us
    pallas_call x1, Pallas kernels, units(): pl.pallas_call(unit_kernel, out_shape=(rows, rows), in_specs=[HBM, HBM],...  2.89 us
  transfers between devices with their start and end apart: 6, of which 3 were waited for; matrix products, arithmetic and copies ran while one was open for 1% of the time, Pallas kernels for 7%

profile of v3, /device:TPU:2, one launch (start us, length us, event | category | flops | bytes accessed | tf_op | source)
XLA Modules:
  0.0 101.7 jit_solution(15538000608889371637)
XLA Ops:
  0.6 2.9 %shard_map.67 = (bf16[256,1152]{1,0:T(8,128)(2,1)}, bf16[256,1152]{1,0:T(8,128)(2,1)}) custom-call(bf16[256,1152]{1,0:T(8,128)(2,1)} %image.7, bf16[256,1152]{1,0:T(8,128)(2,1)} %text.7), custom_call_target="tpu_custom_call" | custom-call | flops 2000000 | bytes 2400000 | tf_op jit(solution)/shard_map/pallas_call | solution.py:103
  3.5 3.5 %collective-permute-start.1 = (bf16[256,1152]{1,0:T(8,128)(2,1)}, bf16[256,1152]{1,0:T(8,128)(2,1)S(1)}, u32[]{:S(2)}, u32[]{:S(2)}) collective-permute-start(bf16[256,1152]{1,0:T(8,128)(2,1)} %get-tuple-element.35.p0), channel_id=1, source_target_pairs={{0,8},{1,761},{2,10},{3,763},{4,12},{5,765},{6,14},{7,767},{8,16},... | collective-permute-start | bytes 1769480 | tf_op jit(solution)/shard_map/ppermute | solution.py:33
  8.3 1.1 %copy-done = bf16[256,1152]{1,0:T(8,128)(2,1)S(1)} copy-done((bf16[256,1152]{1,0:T(8,128)(2,1)S(1)}, bf16[256,1152]{1,0:T(8,128)(2,1)}, u32[]{:S(2)}) %copy-start) | copy-done | bytes 589848
  9.4 1.1 %copy-done.1 = bf16[256,1152]{1,0:T(8,128)(2,1)S(1)} copy-done((bf16[256,1152]{1,0:T(8,128)(2,1)S(1)}, bf16[256,1152]{1,0:T(8,128)(2,1)}, u32[]{:S(2)}) %copy-start.1) | copy-done | bytes 589848
  10.4 0.8 shard_map.68
  11.3 0.7 copy-done.5
  11.9 0.7 copy-done.7
  12.6 7.4 %collective-permute-start = (bf16[256,1152]{1,0:T(8,128)(2,1)S(1)}, bf16[256,1152]{1,0:T(8,128)(2,1)S(1)}, u32[]{:S(2)}, u32[]{:S(2)}) collective-permute-start(bf16[256,1152]{1,0:T(8,128)(2,1)S(1)} %copy-done.1), channel_id=1, source_target_pairs={{0,760},{1,9},{2,762},{3,11},{4,764},{5,13},{6,766},{7,15},{8,0},{... | collective-permute-start | bytes 1769480 | tf_op jit(solution)/shard_map/ppermute | solution.py:33
  20.0 0.6 collective-permute-done.1.p1
  20.6 1.9 %collective-permute-start.2 = (bf16[256,1152]{1,0:T(8,128)(2,1)S(1)}, bf16[256,1152]{1,0:T(8,128)(2,1)S(1)}, u32[]{:S(2)}, u32[]{:S(2)}) collective-permute-start(bf16[256,1152]{1,0:T(8,128)(2,1)S(1)} %collective-permute-done.1.p1), channel_id=1, source_target_pairs={{0,8},{1,761},{2,10},{3,763},{4,12},{5,765},{6,14},{7,767},{8,16},... | collective-permute-start | bytes 1769480 | tf_op jit(solution)/shard_map/ppermute | solution.py:33
  22.5 5.0 %collective-permute-done.q1 = bf16[256,1152]{1,0:T(8,128)(2,1)S(1)} collective-permute-done((bf16[256,1152]{1,0:T(8,128)(2,1)S(1)}, bf16[256,1152]{1,0:T(8,128)(2,1)S(1)}, u32[]{:S(2)}, u32[]{:S(2)}) %collective-permute-start) | collective-permute-done | bytes 589856 | tf_op jit(solution)/shard_map/ppermute | solution.py:33
  27.5 1.1 %shard_map.69 = (bf16[256,256]{1,0:T(8,128)(2,1)S(1)}, bf16[256,256]{1,0:T(8,128)(2,1)S(1)}, f32[24,128]{1,0:T(8,128)S(1)}) custom-call(f32[1]{0:T(128)S(6)} %copy.21.e_ref, f32[1]{0:T(128)S(6)} %copy.22.b_ref, f32[24,128]{1,0:T(8,128)S(1)} %get-tuple-element.38.sums_in, bf16[256,1152]{1,0:T(8,128)(2,1)S(1)} %copy-done, bf16[256,1152]{1,0:T(8,128)(2,1)S(1)} %copy-done.1, ...), custom_call_target="tpu_custom_call" | custom-call | flops 500000000 | bytes 2700000 | tf_op jit(solution)/shard_map/pallas_call | solution.py:162
  28.6 0.6 copy-done.6
  29.2 9.5 %collective-permute-done.2.p2 = bf16[256,1152]{1,0:T(8,128)(2,1)S(1)} collective-permute-done((bf16[256,1152]{1,0:T(8,128)(2,1)S(1)}, bf16[256,1152]{1,0:T(8,128)(2,1)S(1)}, u32[]{:S(2)}, u32[]{:S(2)}) %collective-permute-start.2) | collective-permute-done | bytes 589856 | tf_op jit(solution)/shard_map/ppermute | solution.py:33
  38.7 0.7 shard_map.70
  39.3 1.9 %collective-permute-start.3 = (bf16[256,1152]{1,0:T(8,128)(2,1)S(1)}, bf16[256,1152]{1,0:T(8,128)(2,1)S(1)}, u32[]{:S(2)}, u32[]{:S(2)}) collective-permute-start(bf16[256,1152]{1,0:T(8,128)(2,1)S(1)} %collective-permute-done.q1), channel_id=1, source_target_pairs={{0,760},{1,9},{2,762},{3,11},{4,764},{5,13},{6,766},{7,15},{8,0},{... | collective-permute-start | bytes 1769480 | tf_op jit(solution)/shard_map/ppermute | solution.py:33
  41.3 3.9 %collective-permute-start.5 = (bf16[256,1152]{1,0:T(8,128)(2,1)S(1)}, bf16[256,1152]{1,0:T(8,128)(2,1)S(1)}, u32[]{:S(2)}, u32[]{:S(2)}) collective-permute-start(bf16[256,1152]{1,0:T(8,128)(2,1)S(1)} %collective-permute-done.2.p2), channel_id=1, source_target_pairs={{0,8},{1,761},{2,10},{3,763},{4,12},{5,765},{6,14},{7,767},{8,16},... | collective-permute-start | bytes 1769480 | tf_op jit(solution)/shard_map/ppermute | solution.py:33
  45.2 26.0 %all_to_all.21 = f32[64,1,128]{2,1,0:T(1,128)S(1)} all-to-all(f32[64,1,128]{2,1,0:T(1,128)S(1)} %bitcast.9), channel_id=1, replica_groups=mesh['x'=4,'l'=3,'y'=8,'h'=4,'c'=2] {'x','y','c'}, dimensions={0} | all-to-all | bytes 65536 | tf_op jit(solution)/shard_map/all_to_all | solution.py:380
  71.2 6.2 %collective-permute-start.4 = (bf16[256,1152]{1,0:T(8,128)(2,1)S(1)}, bf16[256,1152]{1,0:T(8,128)(2,1)S(1)}, u32[]{:S(2)}, u32[]{:S(2)}) collective-permute-start(bf16[256,1152]{1,0:T(8,128)(2,1)S(1)} %collective-permute-done.3.q2), channel_id=1, source_target_pairs={{0,760},{1,9},{2,762},{3,11},{4,764},{5,13},{6,766},{7,15},{8,0},{... | collective-permute-start | bytes 1769480 | tf_op jit(solution)/shard_map/ppermute | solution.py:33
  77.5 0.8 copy-done.10
  78.3 5.1 %shard_map.71 = (f32[256,1152]{1,0:T(8,128)}, f32[256,1152]{1,0:T(8,128)}, bf16[256,256]{1,0:T(8,128)(2,1)}) custom-call(f32[1]{0:T(128)S(6)} %copy.21.e_ref, f32[1]{0:T(128)S(6)} %copy.22.b_ref, bf16[256,1152]{1,0:T(8,128)(2,1)} %image.7, bf16[256,1152]{1,0:T(8,128)(2,1)} %text.7, bf16[256,1152]{1,0:T(8,128)(2,1)} %get-tuple-element.35.p0, ...), custom_call_target="tpu_custom_call" | custom-call | flops 1000000000 | bytes 5000000 | tf_op jit(solution)/shard_map/pallas_call | solution.py:323
  83.4 12.5 %all_to_all.22 = f32[12,1,128]{2,1,0:T(1,128)S(1)} all-to-all(f32[12,1,128]{2,1,0:T(1,128)S(1)} %broadcast_in_dim.9), channel_id=1, replica_groups=mesh['x'=4,'l'=3,'y'=8,'h'=4,'c'=2] {'l','h'}, dimensions={0} | all-to-all | bytes 12288 | tf_op jit(solution)/shard_map/all_to_all | solution.py:386
  96.5 0.8 copy-done.11
  97.4 4.3 %shard_map.73 = (f32[256,1152]{1,0:T(8,128)}, f32[256,1152]{1,0:T(8,128)}) custom-call(f32[1]{0:T(128)S(6)} %copy.21.e_ref, f32[1]{0:T(128)S(6)} %copy.22.b_ref, bf16[256,1152]{1,0:T(8,128)(2,1)} %image.7, bf16[256,1152]{1,0:T(8,128)(2,1)} %text.7, bf16[256,1152]{1,0:T(8,128)(2,1)} %get-tuple-element.37.q0, ...), custom_call_target="tpu_custom_call", output_to_operand_aliasing={{0}: (12, {}), {1}: (13, {})} | custom-call | flops 1000000000 | bytes 5000000 | tf_op jit(solution)/shard_map/pallas_call | solution.py:347
  (26 shorter events, 0.7 us)
Async XLA Ops:
  3.5 17.0 %collective-permute-start.1 = (bf16[256,1152]{1,0:T(8,128)(2,1)}, bf16[256,1152]{1,0:T(8,128)(2,1)S(1)}, u32[]{:S(2)}, u32[]{:S(2)}) collective-permute-start(bf16[256,1152]{1,0:T(8,128)(2,1)} %get-tuple-element.35.p0), channel_id=1, source_target_pairs={{0,8},{1,761},{2,10},{3,763},{4,12},{5,765},{6,14},{7,767},{8,16},... | collective-permute-start | bytes 1769480 | tf_op jit(solution)/shard_map/ppermute | solution.py:33
  8.3 1.1 %copy-start = (bf16[256,1152]{1,0:T(8,128)(2,1)S(1)}, bf16[256,1152]{1,0:T(8,128)(2,1)}, u32[]{:S(2)}) copy-start(bf16[256,1152]{1,0:T(8,128)(2,1)} %get-tuple-element.35.p0) | copy-start | bytes 1769476
  9.4 1.1 %copy-start.1 = (bf16[256,1152]{1,0:T(8,128)(2,1)S(1)}, bf16[256,1152]{1,0:T(8,128)(2,1)}, u32[]{:S(2)}) copy-start(bf16[256,1152]{1,0:T(8,128)(2,1)} %get-tuple-element.37.q0) | copy-start | bytes 1769476
  11.3 0.7 copy-start.5
  11.9 0.7 copy-start.7
  12.6 14.9 %collective-permute-start = (bf16[256,1152]{1,0:T(8,128)(2,1)S(1)}, bf16[256,1152]{1,0:T(8,128)(2,1)S(1)}, u32[]{:S(2)}, u32[]{:S(2)}) collective-permute-start(bf16[256,1152]{1,0:T(8,128)(2,1)S(1)} %copy-done.1), channel_id=1, source_target_pairs={{0,760},{1,9},{2,762},{3,11},{4,764},{5,13},{6,766},{7,15},{8,0},{... | collective-permute-start | bytes 1769480 | tf_op jit(solution)/shard_map/ppermute | solution.py:33
  20.6 8.0 %copy-start.3 = (bf16[256,1152]{1,0:T(8,128)(2,1)}, bf16[256,1152]{1,0:T(8,128)(2,1)S(1)}, u32[]{:S(2)}) copy-start(bf16[256,1152]{1,0:T(8,128)(2,1)S(1)} %collective-permute-done.1.p1) | copy-start | bytes 1769476
  20.6 18.1 %collective-permute-start.2 = (bf16[256,1152]{1,0:T(8,128)(2,1)S(1)}, bf16[256,1152]{1,0:T(8,128)(2,1)S(1)}, u32[]{:S(2)}, u32[]{:S(2)}) collective-permute-start(bf16[256,1152]{1,0:T(8,128)(2,1)S(1)} %collective-permute-done.1.p1), channel_id=1, source_target_pairs={{0,8},{1,761},{2,10},{3,763},{4,12},{5,765},{6,14},{7,767},{8,16},... | collective-permute-start | bytes 1769480 | tf_op jit(solution)/shard_map/ppermute | solution.py:33
  27.5 11.9 %copy-start.2 = (bf16[256,1152]{1,0:T(8,128)(2,1)}, bf16[256,1152]{1,0:T(8,128)(2,1)S(1)}, u32[]{:S(2)}) copy-start(bf16[256,1152]{1,0:T(8,128)(2,1)S(1)} %collective-permute-done.q1) | copy-start | bytes 1769476
  28.5 0.6 copy-start.6
  29.2 42.0 %copy-start.8 = (bf16[256,256]{1,0:T(8,128)(2,1)}, bf16[256,256]{1,0:T(8,128)(2,1)S(1)}, u32[]{:S(2)}) copy-start(bf16[256,256]{1,0:T(8,128)(2,1)S(1)} %get-tuple-element.44.d10) | copy-start | bytes 393220
  38.7 38.8 %copy-start.4 = (bf16[256,1152]{1,0:T(8,128)(2,1)}, bf16[256,1152]{1,0:T(8,128)(2,1)S(1)}, u32[]{:S(2)}) copy-start(bf16[256,1152]{1,0:T(8,128)(2,1)S(1)} %collective-permute-done.2.p2) | copy-start | bytes 1769476
  39.3 31.8 %collective-permute-start.3 = (bf16[256,1152]{1,0:T(8,128)(2,1)S(1)}, bf16[256,1152]{1,0:T(8,128)(2,1)S(1)}, u32[]{:S(2)}, u32[]{:S(2)}) collective-permute-start(bf16[256,1152]{1,0:T(8,128)(2,1)S(1)} %collective-permute-done.q1), channel_id=1, source_target_pairs={{0,760},{1,9},{2,762},{3,11},{4,764},{5,13},{6,766},{7,15},{8,0},{... | collective-permute-start | bytes 1769480 | tf_op jit(solution)/shard_map/ppermute | solution.py:33
  41.3 36.2 %collective-permute-start.5 = (bf16[256,1152]{1,0:T(8,128)(2,1)S(1)}, bf16[256,1152]{1,0:T(8,128)(2,1)S(1)}, u32[]{:S(2)}, u32[]{:S(2)}) collective-permute-start(bf16[256,1152]{1,0:T(8,128)(2,1)S(1)} %collective-permute-done.2.p2), channel_id=1, source_target_pairs={{0,8},{1,761},{2,10},{3,763},{4,12},{5,765},{6,14},{7,767},{8,16},... | collective-permute-start | bytes 1769480 | tf_op jit(solution)/shard_map/ppermute | solution.py:33
  71.2 6.3 %copy-start.9 = (bf16[256,1152]{1,0:T(8,128)(2,1)}, bf16[256,1152]{1,0:T(8,128)(2,1)S(1)}, u32[]{:S(2)}) copy-start(bf16[256,1152]{1,0:T(8,128)(2,1)S(1)} %collective-permute-done.3.q2) | copy-start | bytes 1769476
  71.2 25.3 %collective-permute-start.4 = (bf16[256,1152]{1,0:T(8,128)(2,1)S(1)}, bf16[256,1152]{1,0:T(8,128)(2,1)S(1)}, u32[]{:S(2)}, u32[]{:S(2)}) collective-permute-start(bf16[256,1152]{1,0:T(8,128)(2,1)S(1)} %collective-permute-done.3.q2), channel_id=1, source_target_pairs={{0,760},{1,9},{2,762},{3,11},{4,764},{5,13},{6,766},{7,15},{8,0},{... | collective-permute-start | bytes 1769480 | tf_op jit(solution)/shard_map/ppermute | solution.py:33
  77.5 0.8 copy-start.10
  96.5 0.8 copy-start.11

commit v4 on v2

v4 whole, which is shorter than its diff:
```python
import functools

import jax
import jax.numpy as jnp
from jax import lax
from jax.experimental import pallas as pl
from jax.experimental.pallas import tpu as pltpu
from jax.sharding import Mesh, PartitionSpec as P

EPSILON = 1e-06
ROWS, D = 256, 1152
BLK_PARTS = (4, 3, 8)
GRP_PARTS = (4, 2)
N_BLK, N_GRP = 96, 8
AXES = ("x", "l", "y", "h", "c")
BF16, F32 = jnp.bfloat16, jnp.float32
PARAMS = pltpu.CompilerParams(vmem_limit_bytes=16 * 1024 * 1024)
LIGHT = pl.CostEstimate(flops=1000, bytes_accessed=1000, transcendentals=0)
WHOLE = pltpu.CompilerParams(vmem_limit_bytes=60 * 1024 * 1024)
CHUNK = 32
GRAD = jax.ShapeDtypeStruct((ROWS, D), F32)
EARLY_PLANES = 5

SMEM = pl.BlockSpec(memory_space=pltpu.SMEM)
VMEM = pl.BlockSpec(memory_space=pltpu.VMEM)
HBM = pl.BlockSpec(memory_space=pltpu.HBM)


def hop(value, steps):
    pairs = []
    for b in range(N_BLK):
        for g in range(N_GRP):
            way = steps if g % 2 == 0 else -steps
            pairs.append((b * N_GRP + g, ((b + way) % N_BLK) * N_GRP + g))
    return lax.ppermute(value, AXES, pairs)


def cosines(rows, cols):
    return lax.dot_general(rows, cols, (((1,), (1,)), ((), ())), preferred_element_type=F32)


def sigmoid_parts(x):
    small = jnp.exp(-jnp.abs(x))
    return small, jnp.where(x >= 0, 1.0, small) / (1.0 + small)


def folded(values):
    part = values[0:8]
    for r in range(8, ROWS, 8):
        part = part + values[r : r + 8]
    return part[:, 0:128] + part[:, 128:256]


def add_sums(sums_ref, cosine, logit, x, slope, small):
    softplus = jnp.maximum(x, 0.0) + jnp.log1p(small)
    sums_ref[0:8, :] += folded(softplus)
    sums_ref[8:16, :] += folded(slope * cosine)
    sums_ref[16:24, :] += folded(slope)


def logits(cosine, e_ref, b_ref):
    scale = jnp.exp(jnp.full((1, ROWS), e_ref[0], F32))
    return scale * cosine + b_ref[0]


PART = 64


def to_unit(source, out):
    for r in range(0, ROWS, CHUNK):
        v = source[r : r + CHUNK, :].astype(F32)
        inverse = lax.rsqrt(jnp.sum(v * v, axis=-1, keepdims=True) + EPSILON)
        out[r : r + CHUNK, :] = (v * inverse).astype(BF16)


def unit_kernel(image, text, p0, q0):
    even = lax.axis_index("c") == 0

    @pl.when(even)
    def _():
        to_unit(text, p0)
        to_unit(image, q0)

    @pl.when(jnp.logical_not(even))
    def _():
        to_unit(image, p0)
        to_unit(text, q0)


def units(image, text):
    rows = jax.ShapeDtypeStruct((ROWS, D), BF16)
    return pl.pallas_call(
        unit_kernel,
        out_shape=(rows, rows),
        in_specs=[VMEM, VMEM],
        out_specs=(VMEM, VMEM),
        compiler_params=PARAMS,
        cost_estimate=LIGHT,
    )(image, text)


def own_kernel(e_ref, b_ref, p0, q0, d00, d00t, sums):
    i = lax.broadcasted_iota(jnp.int32, (ROWS, ROWS), 0)
    j = lax.broadcasted_iota(jnp.int32, (ROWS, ROWS), 1)
    pair = i == j
    sums[...] = jnp.zeros_like(sums)
    cosine = cosines(q0[...], p0[...])
    logit = logits(cosine, e_ref, b_ref)
    x = jnp.where(pair, -logit, logit)
    small, sig = sigmoid_parts(x)
    slope = jnp.where(pair, -sig, sig)
    add_sums(sums, cosine, logit, x, slope, small)
    d00[...] = slope.astype(BF16)
    logit = logits(cosines(p0[...], q0[...]), e_ref, b_ref)
    _, sig = sigmoid_parts(jnp.where(pair, -logit, logit))
    d00t[...] = jnp.where(pair, -sig, sig).astype(BF16)


def own(e, b, p0, q0):
    return pl.pallas_call(
        own_kernel,
        out_shape=(
            jax.ShapeDtypeStruct((ROWS, ROWS), BF16),
            jax.ShapeDtypeStruct((ROWS, ROWS), BF16),
            jax.ShapeDtypeStruct((24, 128), F32),
        ),
        in_specs=[SMEM, SMEM, VMEM, VMEM],
        out_specs=(VMEM, VMEM, VMEM),
        compiler_params=PARAMS,
        cost_estimate=LIGHT,
    )(e, b, p0, q0)


def grid_sums(e_ref, b_ref, rows, cols, sums):
    cosine = cosines(rows, cols)
    logit = logits(cosine, e_ref, b_ref)
    small, slope = sigmoid_parts(logit)
    add_sums(sums, cosine, logit, logit, slope, small)
    return slope.astype(BF16)


def middle_kernel(e_ref, b_ref, sums_in, p0, q0, p1, q1, d00, d00t, sums, g_q, g_p):
    sums[...] = sums_in[...]
    d01 = grid_sums(e_ref, b_ref, q0[...], p1[...], sums)
    grid_sums(e_ref, b_ref, q1[...], p1[...], sums)
    g_q[...] = jnp.dot(d00[...], p0[...], preferred_element_type=F32)
    g_q[...] += jnp.dot(d01, p1[...], preferred_element_type=F32)
    d10 = slope_block(e_ref, b_ref, p0[...], q1[...])
    g_p[...] = jnp.dot(d00t[...], q0[...], preferred_element_type=F32)
    g_p[...] += jnp.dot(d10, q1[...], preferred_element_type=F32)


def middle(e, b, sums, p0, q0, p1, q1, d00, d00t):
    return pl.pallas_call(
        middle_kernel,
        out_shape=(jax.ShapeDtypeStruct((24, 128), F32), GRAD, GRAD),
        in_specs=[SMEM, SMEM] + [VMEM] * 7,
        out_specs=(VMEM, VMEM, VMEM),
        compiler_params=PARAMS,
        cost_estimate=LIGHT,
    )(e, b, sums, p0, q0, p1, q1, d00, d00t)


def last_kernel(e_ref, b_ref, sums_in, q1, p2, out, sums):
    sums[...] = sums_in[...]
    grid_sums(e_ref, b_ref, q1[...], p2[...], sums)
    scale = jnp.exp(jnp.full((1, 1), e_ref[0], F32))
    loss = jnp.sum(sums[0:8, :], keepdims=True)
    by_scale = scale * jnp.sum(sums[8:16, :], keepdims=True)
    by_bias = jnp.sum(sums[16:24, :], keepdims=True)
    lane = lax.broadcasted_iota(jnp.int32, out.shape, 1)
    row = jnp.where(lane == 0, loss, jnp.where(lane == 1, by_scale, jnp.where(lane == 2, by_bias, 0.0)))
    out[...] = row


def last(e, b, sums, q1, p2, count):
    return pl.pallas_call(
        last_kernel,
        out_shape=jax.ShapeDtypeStruct((count, 128), F32),
        in_specs=[SMEM, SMEM] + [VMEM] * 3,
        out_specs=VMEM,
        scratch_shapes=[pltpu.VMEM((24, 128), F32)],
        compiler_params=PARAMS,
        cost_estimate=LIGHT,
    )(e, b, sums, q1, p2)


def started(pairs, sems):
    copies = [pltpu.make_async_copy(src, dst, sems.at[n]) for n, (src, dst) in enumerate(pairs)]
    for copy in copies:
        copy.start()
    return copies


def either(chosen, first, second):
    @pl.when(chosen)
    def _():
        first.start()

    @pl.when(jnp.logical_not(chosen))
    def _():
        second.start()


def inverse_norm(v):
    return lax.rsqrt(jnp.sum(v * v, axis=-1, keepdims=True) + EPSILON)


def finish(e_ref, total, raw, out, is_text, out_image, out_text, sem):
    scale = jnp.exp(jnp.full((1, 1), e_ref[0], F32))
    for r in range(0, ROWS, CHUNK):
        rows = slice(r, r + CHUNK)
        v = raw[rows, :].astype(F32)
        inverse = inverse_norm(v)
        u = v * inverse
        g = scale * total[rows, :]
        out[rows, :] = inverse * (g - u * jnp.sum(u * g, axis=-1, keepdims=True))
        if (r + CHUNK) % PART == 0:
            part = pl.ds(r + CHUNK - PART, PART)
            either(
                is_text,
                pltpu.make_async_copy(out.at[part, :], out_text.at[part, :], sem),
                pltpu.make_async_copy(out.at[part, :], out_image.at[part, :], sem),
            )


def slope_block(e_ref, b_ref, rows, cols):
    return sigmoid_parts(logits(cosines(rows, cols), e_ref, b_ref))[1].astype(BF16)


def load_raw(is_text, image, text, raw, sem):
    from_text = pltpu.make_async_copy(text, raw, sem)
    either(is_text, from_text, pltpu.make_async_copy(image, raw, sem))
    return from_text


def side_kernel(side, when, e_ref, b_ref, image, text, near, far2, far3, *refs):
    out_image, out_text, total, raw, out, own, far, d, sems, out_sem = refs if when == "early" else refs[2:]
    early = 3 * lax.axis_index("h") + lax.axis_index("l") < EARLY_PLANES
    is_text = lax.axis_index("c") == 1 - side

    def work():
        raw_copy = load_raw(is_text, image, text, raw, sems.at[3])
        copies = started([(far2, far.at[pl.ds(0, ROWS), :]), (far3, far.at[pl.ds(ROWS, ROWS), :]), (near, total)], sems)
        raw_copy.wait()
        for r in range(0, ROWS, CHUNK):
            v = raw[r : r + CHUNK, :].astype(F32)
            own[r : r + CHUNK, :] = (v * inverse_norm(v)).astype(BF16)
        for n in range(2):
            copies[n].wait()
            rows = pl.ds(n * ROWS, ROWS)
            d[:, rows] = slope_block(e_ref, b_ref, own[...], far[rows, :])
        copies[2].wait()
        total[...] += jnp.dot(d[...], far[...], preferred_element_type=F32)
        finish(e_ref, total, raw, out, is_text, out_image, out_text, out_sem)
        pltpu.make_async_copy(out, out_text, out_sem).wait()

    if when == "always":
        work()
    else:
        pl.when(early if when == "early" else jnp.logical_not(early))(work)


def one_side(side, when, args, previous=()):
    n = len(args)
    return pl.pallas_call(
        functools.partial(side_kernel, side, when),
        out_shape=(GRAD, GRAD),
        in_specs=[SMEM, SMEM] + [HBM] * (n - 2 + len(previous)),
        out_specs=(HBM, HBM),
        input_output_aliases={n: 0, n + 1: 1} if previous else {},
        scratch_shapes=[
            pltpu.VMEM((ROWS, D), F32),
            pltpu.VMEM((ROWS, D), BF16),
            pltpu.VMEM((ROWS, D), F32),
            pltpu.VMEM((ROWS, D), BF16),
            pltpu.VMEM((2 * ROWS, D), BF16),
            pltpu.VMEM((ROWS, 2 * ROWS), BF16),
            pltpu.SemaphoreType.DMA((4,)),
            pltpu.SemaphoreType.DMA,
        ],
        compiler_params=WHOLE,
        cost_estimate=LIGHT,
    )(*args, *previous)


def body(image, text, e, b):
    bar = lax.optimization_barrier
    p0, q0 = units(image, text)
    p1 = hop(p0, 1)
    d00, d00t, sums = own(e, b, p0, q0)
    sums, q0s = bar((sums, q0))
    q1 = hop(q0s, -1)
    p2 = hop(p1, 1)
    sums, g_q, g_p = middle(e, b, sums, p0, q0, p1, q1, d00, d00t)
    sums, q1s = bar((sums, q1))
    q2 = hop(q1s, -1)
    row = last(e, b, sums, q1, p2, 64)
    row, p2s = bar((row, p2))
    p3 = hop(p2s, 1)
    row = lax.all_to_all(row, ("x", "y", "c"), 0, 0, tiled=True)
    row, q2 = bar((row, q2))
    q3 = hop(q2, -1)
    row, p3 = bar((jnp.sum(row, axis=0, keepdims=True), p3))
    q_args = (e, b, image, text, g_q, p2, p3)
    row, done = bar((row, one_side(0, "early", q_args)))
    row = lax.all_to_all(jnp.broadcast_to(row, (12, 128)), ("l", "h"), 0, 0, tiled=True)
    row, done = bar((row, done))
    totals = jnp.sum(row, axis=0)[:3] / jnp.float32(ROWS * N_BLK * N_GRP)
    done = one_side(0, "late", q_args, done)
    grad_image, grad_text = one_side(1, "always", (e, b, image, text, g_p, q2, q3), done)
    return grad_image, grad_text, totals


def solution(mesh):
    fine = Mesh(mesh.devices.reshape(BLK_PARTS + GRP_PARTS), AXES)
    split = P(AXES, None)
    return jax.shard_map(
        body,
        mesh=fine,
        in_specs=(split, split, P(), P()),
        out_specs=(split, split, P()),
        check_vma=False,
    )
```

time: 113 us -> 97.7 us (0.86)
  the two profiles are of different devices: /device:TPU:128 before, /device:TPU:2 now
where the time goes in v4:
time: 97.7 us; the launch traced here: 97.2 us
  starting transfers between devices  46.7 us (48%)
  waiting for transfers between devices  16.9 us (17%)
  Pallas kernels  12.7 us (13%)
  blocking collectives  12.5 us (13%)
  local copies, waits for them, and re-layouts  5.81 us (6%)
  between operations  2.11 us (2%)
    ppermute x6, starting transfers between devices, hop(): return lax.ppermute(value, AXES, pairs)  29.3 us
    all_to_all x1, starting transfers between devices, body(): row = lax.all_to_all(row, ('x', 'y', 'c'), 0, 0, tiled=True)  17.3 us
    all_to_all x1, blocking collectives, body(): lax.all_to_all(jnp.broadcast_to(row, (12, 128)), ('l', 'h'), 0, 0, tiled=...  12.5 us
    all_to_all x1, waiting for transfers between devices, body(): row = lax.all_to_all(row, ('x', 'y', 'c'), 0, 0, tiled=True)  10.3 us
    pallas_call x3, Pallas kernels, one_side(): pl.pallas_call(functools.partial(side_kernel, side, when), out_shape=(GRA...  8.2 us
    ppermute x6, waiting for transfers between devices, hop(): return lax.ppermute(value, AXES, pairs)  6.59 us
    unnamed x17, local copies, waits for them, and re-layouts  5.8 us
    pallas_call x1, Pallas kernels, middle(): pl.pallas_call(middle_kernel, out_shape=(jax.ShapeDtypeStruct((24, 128),...  1.97 us
  transfers between devices with their start and end apart: 7, of which 3 were waited for; matrix products, arithmetic and copies ran while one was open for 1% of the time, Pallas kernels for 8%

profile of v4, /device:TPU:2, one launch (start us, length us, event | category | flops | bytes accessed | tf_op | source)
XLA Modules:
  0.0 97.2 jit_solution(402517451454229436)
XLA Ops:
  0.6 1.1 %copy-done = bf16[256,1152]{1,0:T(8,128)(2,1)S(1)} copy-done((bf16[256,1152]{1,0:T(8,128)(2,1)S(1)}, bf16[256,1152]{1,0:T(8,128)(2,1)}, u32[]{:S(2)}) %copy-start) | copy-done | bytes 589848
  1.7 1.1 %copy-done.1 = bf16[256,1152]{1,0:T(8,128)(2,1)S(1)} copy-done((bf16[256,1152]{1,0:T(8,128)(2,1)S(1)}, bf16[256,1152]{1,0:T(8,128)(2,1)}, u32[]{:S(2)}) %copy-start.1) | copy-done | bytes 589848
  2.8 0.4 shard_map.67
  3.1 3.5 %collective-permute-start = (bf16[256,1152]{1,0:T(8,128)(2,1)S(1)}, bf16[256,1152]{1,0:T(8,128)(2,1)S(1)}, u32[]{:S(2)}, u32[]{:S(2)}) collective-permute-start(bf16[256,1152]{1,0:T(8,128)(2,1)S(1)} %get-tuple-element.33.p0), channel_id=1, source_target_pairs={{0,8},{1,761},{2,10},{3,763},{4,12},{5,765},{6,14},{7,767},{8,16},... | collective-permute-start | bytes 1769480 | tf_op jit(solution)/shard_map/ppermute | solution.py:35
  7.9 0.8 shard_map.68
  8.8 7.4 %collective-permute-start.1 = (bf16[256,1152]{1,0:T(8,128)(2,1)S(1)}, bf16[256,1152]{1,0:T(8,128)(2,1)S(1)}, u32[]{:S(2)}, u32[]{:S(2)}) collective-permute-start(bf16[256,1152]{1,0:T(8,128)(2,1)S(1)} %get-tuple-element.37.q0), channel_id=1, source_target_pairs={{0,760},{1,9},{2,762},{3,11},{4,764},{5,13},{6,766},{7,15},{8,0},{... | collective-permute-start | bytes 1769480 | tf_op jit(solution)/shard_map/ppermute | solution.py:35
  16.2 3.8 %collective-permute-done.p1 = bf16[256,1152]{1,0:T(8,128)(2,1)S(1)} collective-permute-done((bf16[256,1152]{1,0:T(8,128)(2,1)S(1)}, bf16[256,1152]{1,0:T(8,128)(2,1)S(1)}, u32[]{:S(2)}, u32[]{:S(2)}) %collective-permute-start) | collective-permute-done | bytes 589856 | tf_op jit(solution)/shard_map/ppermute | solution.py:35
  20.0 1.9 %collective-permute-start.2 = (bf16[256,1152]{1,0:T(8,128)(2,1)S(1)}, bf16[256,1152]{1,0:T(8,128)(2,1)S(1)}, u32[]{:S(2)}, u32[]{:S(2)}) collective-permute-start(bf16[256,1152]{1,0:T(8,128)(2,1)S(1)} %collective-permute-done.p1), channel_id=1, source_target_pairs={{0,8},{1,761},{2,10},{3,763},{4,12},{5,765},{6,14},{7,767},{8,16},... | collective-permute-start | bytes 1769480 | tf_op jit(solution)/shard_map/ppermute | solution.py:35
  21.9 2.8 %collective-permute-done.1.q1 = bf16[256,1152]{1,0:T(8,128)(2,1)S(1)} collective-permute-done((bf16[256,1152]{1,0:T(8,128)(2,1)S(1)}, bf16[256,1152]{1,0:T(8,128)(2,1)S(1)}, u32[]{:S(2)}, u32[]{:S(2)}) %collective-permute-start.1) | collective-permute-done | bytes 589856 | tf_op jit(solution)/shard_map/ppermute | solution.py:35
  24.7 2.0 %shard_map.69 = (f32[24,128]{1,0:T(8,128)S(1)}, f32[256,1152]{1,0:T(8,128)S(1)}, f32[256,1152]{1,0:T(8,128)S(1)}) custom-call(f32[1]{0:T(128)S(6)} %copy.19.e_ref, f32[1]{0:T(128)S(6)} %copy.20.b_ref, f32[24,128]{1,0:T(8,128)S(1)} %get-tuple-element.36.sums_in, bf16[256,1152]{1,0:T(8,128)(2,1)S(1)} %get-tuple-element.33.p0, ...), custom_call_target="tpu_custom_call" | custom-call | flops 1000 | bytes 1000 | tf_op jit(solution)/shard_map/pallas_call | solution.py:154
  26.7 1.0 %copy-done.3 = f32[256,1152]{1,0:T(8,128)} copy-done((f32[256,1152]{1,0:T(8,128)}, f32[256,1152]{1,0:T(8,128)S(1)}, u32[]{:S(2)}) %copy-start.3) | copy-done | bytes 1179672
  27.7 1.0 %copy-done.4 = f32[256,1152]{1,0:T(8,128)} copy-done((f32[256,1152]{1,0:T(8,128)}, f32[256,1152]{1,0:T(8,128)S(1)}, u32[]{:S(2)}) %copy-start.4) | copy-done | bytes 1179672
  28.7 8.3 %collective-permute-start.3 = (bf16[256,1152]{1,0:T(8,128)(2,1)S(1)}, bf16[256,1152]{1,0:T(8,128)(2,1)S(1)}, u32[]{:S(2)}, u32[]{:S(2)}) collective-permute-start(bf16[256,1152]{1,0:T(8,128)(2,1)S(1)} %collective-permute-done.1.q1), channel_id=1, source_target_pairs={{0,760},{1,9},{2,762},{3,11},{4,764},{5,13},{6,766},{7,15},{8,0},{... | collective-permute-start | bytes 1769480 | tf_op jit(solution)/shard_map/ppermute | solution.py:35
  37.0 1.3 %shard_map.70 = f32[64,128]{1,0:T(8,128)} custom-call(f32[1]{0:T(128)S(6)} %copy.19.e_ref, f32[1]{0:T(128)S(6)} %copy.20.b_ref, f32[24,128]{1,0:T(8,128)S(1)} %get-tuple-element.42.sums_in, bf16[256,1152]{1,0:T(8,128)(2,1)S(1)} %collective-permute-done.1.q1, bf16[256,1152]{1,0:T(8,128)(2,1)S(1)} %collective-permute-done.2.p2.far2), custom_call_target="tpu_custom_call" | custom-call | flops 1000 | bytes 1000 | tf_op jit(solution)/shard_map/pallas_call | solution.py:177
  38.3 1.9 %collective-permute-start.5 = (bf16[256,1152]{1,0:T(8,128)(2,1)S(1)}, bf16[256,1152]{1,0:T(8,128)(2,1)S(1)}, u32[]{:S(2)}, u32[]{:S(2)}) collective-permute-start(bf16[256,1152]{1,0:T(8,128)(2,1)S(1)} %collective-permute-done.2.p2.far2), channel_id=1, source_target_pairs={{0,8},{1,761},{2,10},{3,763},{4,12},{5,765},{6,14},{7,767},{8,16},... | collective-permute-start | bytes 1769480 | tf_op jit(solution)/shard_map/ppermute | solution.py:35
  40.2 17.3 %all-to-all-start = ((f32[64,1,128]{2,1,0:T(1,128)}), f32[64,1,128]{2,1,0:T(1,128)S(1)}, u32[]{:S(2)}, u32[]{:S(2)}) async-start(f32[64,1,128]{2,1,0:T(1,128)} %bitcast.1), calls=%async_computation | async-start | bytes 65536 | tf_op jit(solution)/shard_map/all_to_all | solution.py:301
  57.6 10.3 %all-to-all-done = f32[64,1,128]{2,1,0:T(1,128)S(1)} async-done(((f32[64,1,128]{2,1,0:T(1,128)}), f32[64,1,128]{2,1,0:T(1,128)S(1)}, u32[]{:S(2)}, u32[]{:S(2)}) %all-to-all-start) | async-done | bytes 32800 | tf_op jit(solution)/shard_map/all_to_all | solution.py:301
  67.9 6.4 %collective-permute-start.4 = (bf16[256,1152]{1,0:T(8,128)(2,1)S(1)}, bf16[256,1152]{1,0:T(8,128)(2,1)S(1)}, u32[]{:S(2)}, u32[]{:S(2)}) collective-permute-start(bf16[256,1152]{1,0:T(8,128)(2,1)S(1)} %collective-permute-done.3.far2), channel_id=1, source_target_pairs={{0,760},{1,9},{2,762},{3,11},{4,764},{5,13},{6,766},{7,15},{8,0},{... | collective-permute-start | bytes 1769480 | tf_op jit(solution)/shard_map/ppermute | solution.py:35
  74.3 0.8 copy-done.5
  75.1 4.1 %shard_map.71 = (f32[256,1152]{1,0:T(8,128)}, f32[256,1152]{1,0:T(8,128)}) custom-call(f32[1]{0:T(128)S(6)} %copy.19.e_ref, f32[1]{0:T(128)S(6)} %copy.20.b_ref, bf16[256,1152]{1,0:T(8,128)(2,1)} %image.7, bf16[256,1152]{1,0:T(8,128)(2,1)} %text.7, f32[256,1152]{1,0:T(8,128)} %copy-done.3, bf16[256,1152]{1,0:T(8,128)(2,1)} %copy-done.2, ...), custom_call_target="tpu_custom_call" | custom-call | flops 1000 | bytes 1000 | tf_op jit(solution)/shard_map/pallas_call | solution.py:266
  79.2 12.5 %all_to_all.21 = f32[12,1,128]{2,1,0:T(1,128)S(1)} all-to-all(f32[12,1,128]{2,1,0:T(1,128)S(1)} %broadcast_in_dim.9), channel_id=1, replica_groups=mesh['x'=4,'l'=3,'y'=8,'h'=4,'c'=2] {'l','h'}, dimensions={0} | all-to-all | bytes 12288 | tf_op jit(solution)/shard_map/all_to_all | solution.py:307
  91.8 0.5 slice_multiply_fusion
  92.3 0.8 copy-done.7
  93.1 4.1 %shard_map.73 = (f32[256,1152]{1,0:T(8,128)}, f32[256,1152]{1,0:T(8,128)}) custom-call(f32[1]{0:T(128)S(6)} %copy.19.e_ref, f32[1]{0:T(128)S(6)} %copy.20.b_ref, bf16[256,1152]{1,0:T(8,128)(2,1)} %image.7, bf16[256,1152]{1,0:T(8,128)(2,1)} %text.7, f32[256,1152]{1,0:T(8,128)} %copy-done.4, ...), custom_call_target="tpu_custom_call", output_to_operand_aliasing={{0}: (7, {}), {1}: (8, {})} | custom-call | flops 1000 | bytes 1000 | tf_op jit(solution)/shard_map/pallas_call | solution.py:266
  (19 shorter events, 0.1 us)
Async XLA Ops:
  0.6 1.1 %copy-start = (bf16[256,1152]{1,0:T(8,128)(2,1)S(1)}, bf16[256,1152]{1,0:T(8,128)(2,1)}, u32[]{:S(2)}) copy-start(bf16[256,1152]{1,0:T(8,128)(2,1)} %image.7) | copy-start | bytes 1769476
  1.7 1.1 %copy-start.1 = (bf16[256,1152]{1,0:T(8,128)(2,1)S(1)}, bf16[256,1152]{1,0:T(8,128)(2,1)}, u32[]{:S(2)}) copy-start(bf16[256,1152]{1,0:T(8,128)(2,1)} %text.7) | copy-start | bytes 1769476
  3.1 16.8 %collective-permute-start = (bf16[256,1152]{1,0:T(8,128)(2,1)S(1)}, bf16[256,1152]{1,0:T(8,128)(2,1)S(1)}, u32[]{:S(2)}, u32[]{:S(2)}) collective-permute-start(bf16[256,1152]{1,0:T(8,128)(2,1)S(1)} %get-tuple-element.33.p0), channel_id=1, source_target_pairs={{0,8},{1,761},{2,10},{3,763},{4,12},{5,765},{6,14},{7,767},{8,16},... | collective-permute-start | bytes 1769480 | tf_op jit(solution)/shard_map/ppermute | solution.py:35
  8.8 15.9 %collective-permute-start.1 = (bf16[256,1152]{1,0:T(8,128)(2,1)S(1)}, bf16[256,1152]{1,0:T(8,128)(2,1)S(1)}, u32[]{:S(2)}, u32[]{:S(2)}) collective-permute-start(bf16[256,1152]{1,0:T(8,128)(2,1)S(1)} %get-tuple-element.37.q0), channel_id=1, source_target_pairs={{0,760},{1,9},{2,762},{3,11},{4,764},{5,13},{6,766},{7,15},{8,0},{... | collective-permute-start | bytes 1769480 | tf_op jit(solution)/shard_map/ppermute | solution.py:35
  20.0 17.0 %collective-permute-start.2 = (bf16[256,1152]{1,0:T(8,128)(2,1)S(1)}, bf16[256,1152]{1,0:T(8,128)(2,1)S(1)}, u32[]{:S(2)}, u32[]{:S(2)}) collective-permute-start(bf16[256,1152]{1,0:T(8,128)(2,1)S(1)} %collective-permute-done.p1), channel_id=1, source_target_pairs={{0,8},{1,761},{2,10},{3,763},{4,12},{5,765},{6,14},{7,767},{8,16},... | collective-permute-start | bytes 1769480 | tf_op jit(solution)/shard_map/ppermute | solution.py:35
  26.6 1.0 %copy-start.3 = (f32[256,1152]{1,0:T(8,128)}, f32[256,1152]{1,0:T(8,128)S(1)}, u32[]{:S(2)}) copy-start(f32[256,1152]{1,0:T(8,128)S(1)} %get-tuple-element.46.near) | copy-start | bytes 3538948
  27.7 1.0 %copy-start.4 = (f32[256,1152]{1,0:T(8,128)}, f32[256,1152]{1,0:T(8,128)S(1)}, u32[]{:S(2)}) copy-start(f32[256,1152]{1,0:T(8,128)S(1)} %get-tuple-element.40.near) | copy-start | bytes 3538948
  28.7 28.9 %collective-permute-start.3 = (bf16[256,1152]{1,0:T(8,128)(2,1)S(1)}, bf16[256,1152]{1,0:T(8,128)(2,1)S(1)}, u32[]{:S(2)}, u32[]{:S(2)}) collective-permute-start(bf16[256,1152]{1,0:T(8,128)(2,1)S(1)} %collective-permute-done.1.q1), channel_id=1, source_target_pairs={{0,760},{1,9},{2,762},{3,11},{4,764},{5,13},{6,766},{7,15},{8,0},{... | collective-permute-start | bytes 1769480 | tf_op jit(solution)/shard_map/ppermute | solution.py:35
  37.0 37.3 %copy-start.2 = (bf16[256,1152]{1,0:T(8,128)(2,1)}, bf16[256,1152]{1,0:T(8,128)(2,1)S(1)}, u32[]{:S(2)}) copy-start(bf16[256,1152]{1,0:T(8,128)(2,1)S(1)} %collective-permute-done.2.p2.far2) | copy-start | bytes 1769476
  38.3 36.0 %collective-permute-start.5 = (bf16[256,1152]{1,0:T(8,128)(2,1)S(1)}, bf16[256,1152]{1,0:T(8,128)(2,1)S(1)}, u32[]{:S(2)}, u32[]{:S(2)}) collective-permute-start(bf16[256,1152]{1,0:T(8,128)(2,1)S(1)} %collective-permute-done.2.p2.far2), channel_id=1, source_target_pairs={{0,8},{1,761},{2,10},{3,763},{4,12},{5,765},{6,14},{7,767},{8,16},... | collective-permute-start | bytes 1769480 | tf_op jit(solution)/shard_map/ppermute | solution.py:35
  40.2 27.7 %all-to-all-start = ((f32[64,1,128]{2,1,0:T(1,128)}), f32[64,1,128]{2,1,0:T(1,128)S(1)}, u32[]{:S(2)}, u32[]{:S(2)}) async-start(f32[64,1,128]{2,1,0:T(1,128)} %bitcast.1), calls=%async_computation | async-start | bytes 65536 | tf_op jit(solution)/shard_map/all_to_all | solution.py:301
  57.6 34.2 %copy-start.6 = (bf16[256,1152]{1,0:T(8,128)(2,1)}, bf16[256,1152]{1,0:T(8,128)(2,1)S(1)}, u32[]{:S(2)}) copy-start(bf16[256,1152]{1,0:T(8,128)(2,1)S(1)} %collective-permute-done.3.far2) | copy-start | bytes 1769476
  67.9 24.4 %collective-permute-start.4 = (bf16[256,1152]{1,0:T(8,128)(2,1)S(1)}, bf16[256,1152]{1,0:T(8,128)(2,1)S(1)}, u32[]{:S(2)}, u32[]{:S(2)}) collective-permute-start(bf16[256,1152]{1,0:T(8,128)(2,1)S(1)} %collective-permute-done.3.far2), channel_id=1, source_target_pairs={{0,760},{1,9},{2,762},{3,11},{4,764},{5,13},{6,766},{7,15},{8,0},{... | collective-permute-start | bytes 1769480 | tf_op jit(solution)/shard_map/ppermute | solution.py:35
  74.3 0.8 copy-start.5
  92.3 0.8 copy-start.7

commit v5 on v4

--- a/solution.py
+++ b/solution.py
@@ -16,7 +16,7 @@
 BF16, F32 = jnp.bfloat16, jnp.float32
 PARAMS = pltpu.CompilerParams(vmem_limit_bytes=16 * 1024 * 1024)
 LIGHT = pl.CostEstimate(flops=1000, bytes_accessed=1000, transcendentals=0)
-WHOLE = pltpu.CompilerParams(vmem_limit_bytes=60 * 1024 * 1024)
+WHOLE = pltpu.CompilerParams(vmem_limit_bytes=62 * 1024 * 1024)
 CHUNK = 32
 GRAD = jax.ShapeDtypeStruct((ROWS, D), F32)
 EARLY_PLANES = 5
@@ -164,10 +164,11 @@
 def last_kernel(e_ref, b_ref, sums_in, q1, p2, out, sums):
     sums[...] = sums_in[...]
     grid_sums(e_ref, b_ref, q1[...], p2[...], sums)
+    share = 1.0 / (ROWS * N_BLK * N_GRP)
     scale = jnp.exp(jnp.full((1, 1), e_ref[0], F32))
-    loss = jnp.sum(sums[0:8, :], keepdims=True)
-    by_scale = scale * jnp.sum(sums[8:16, :], keepdims=True)
-    by_bias = jnp.sum(sums[16:24, :], keepdims=True)
+    loss = share * jnp.sum(sums[0:8, :], keepdims=True)
+    by_scale = share * scale * jnp.sum(sums[8:16, :], keepdims=True)
+    by_bias = share * jnp.sum(sums[16:24, :], keepdims=True)
     lane = lax.broadcasted_iota(jnp.int32, out.shape, 1)
     row = jnp.where(lane == 0, loss, jnp.where(lane == 1, by_scale, jnp.where(lane == 2, by_bias, 0.0)))
     out[...] = row
@@ -295,18 +296,18 @@
     sums, g_q, g_p = middle(e, b, sums, p0, q0, p1, q1, d00, d00t)
     sums, q1s = bar((sums, q1))
     q2 = hop(q1s, -1)
-    row = last(e, b, sums, q1, p2, 64)
+    row = last(e, b, sums, q1, p2, 16)
     row, p2s = bar((row, p2))
     p3 = hop(p2s, 1)
-    row = lax.all_to_all(row, ("x", "y", "c"), 0, 0, tiled=True)
+    row = lax.all_to_all(row, ("y", "c"), 0, 0, tiled=True)
     row, q2 = bar((row, q2))
     q3 = hop(q2, -1)
     row, p3 = bar((jnp.sum(row, axis=0, keepdims=True), p3))
     q_args = (e, b, image, text, g_q, p2, p3)
     row, done = bar((row, one_side(0, "early", q_args)))
-    row = lax.all_to_all(jnp.broadcast_to(row, (12, 128)), ("l", "h"), 0, 0, tiled=True)
+    row = lax.all_to_all(jnp.broadcast_to(row, (48, 128)), ("x", "l", "h"), 0, 0, tiled=True)
     row, done = bar((row, done))
-    totals = jnp.sum(row, axis=0)[:3] / jnp.float32(ROWS * N_BLK * N_GRP)
+    totals = jnp.sum(row[:, :3], axis=0)
     done = one_side(0, "late", q_args, done)
     grad_image, grad_text = one_side(1, "always", (e, b, image, text, g_p, q2, q3), done)
     return grad_image, grad_text, totals

time: 97.7 us -> 96.5 us (0.988)
  blocking collectives: 12.5 us -> 28.9 us
  starting transfers between devices: 46.7 us -> 32.6 us
  waiting for transfers between devices: 16.9 us -> 14.2 us
    all_to_all x1, blocking collectives: 12.5 us -> 28.9 us  [body(): lax.all_to_all(jnp.broadcast_to(row, (48, 128)), ('x', 'l', 'h'), 0, 0, t...]
    all_to_all x1, starting transfers between devices: 17.3 us -> 4.51 us  [body(): row = lax.all_to_all(row, ('y', 'c'), 0, 0, tiled=True)]
    all_to_all x1, waiting for transfers between devices: 10.3 us -> 7.35 us  [body(): row = lax.all_to_all(row, ('y', 'c'), 0, 0, tiled=True)]
    ppermute x6, starting transfers between devices: 29.3 us -> 28.1 us  [hop(): return lax.ppermute(value, AXES, pairs)]
    unnamed x17 -> x14, local copies, waits for them, and re-layouts: 5.8 us -> 4.98 us
  transfers between devices with their start and end apart: 7 -> 7, of which waited for: 3 -> 4; matrix products, arithmetic and copies ran while one was open for 1% -> 1% of each run, Pallas kernels for 8% -> 9%
where the time goes in v5:
time: 96.5 us; the launch traced here: 96 us
  starting transfers between devices  32.6 us (34%)
  blocking collectives  28.9 us (30%)
  waiting for transfers between devices  14.2 us (15%)
  Pallas kernels  12.6 us (13%)
  local copies, waits for them, and re-layouts  4.99 us (5%)
  between operations  2.09 us (2%)
    all_to_all x1, blocking collectives, body(): lax.all_to_all(jnp.broadcast_to(row, (48, 128)), ('x', 'l', 'h'), 0, 0, t...  28.9 us
    ppermute x6, starting transfers between devices, hop(): return lax.ppermute(value, AXES, pairs)  28.1 us
    pallas_call x3, Pallas kernels, one_side(): pl.pallas_call(functools.partial(side_kernel, side, when), out_shape=(GRA...  8.2 us
    all_to_all x1, waiting for transfers between devices, body(): row = lax.all_to_all(row, ('y', 'c'), 0, 0, tiled=True)  7.35 us
    ppermute x6, waiting for transfers between devices, hop(): return lax.ppermute(value, AXES, pairs)  6.86 us
    unnamed x14, local copies, waits for them, and re-layouts  4.98 us
    all_to_all x1, starting transfers between devices, body(): row = lax.all_to_all(row, ('y', 'c'), 0, 0, tiled=True)  4.51 us
    pallas_call x1, Pallas kernels, middle(): pl.pallas_call(middle_kernel, out_shape=(jax.ShapeDtypeStruct((24, 128),...  1.97 us
  transfers between devices with their start and end apart: 7, of which 4 were waited for; matrix products, arithmetic and copies ran while one was open for 1% of the time, Pallas kernels for 9%

profile of v5, /device:TPU:2, one launch (start us, length us, event | category | flops | bytes accessed | tf_op | source)
XLA Modules:
  0.0 96.0 jit_solution(5150378962103704367)
XLA Ops:
  0.6 1.1 %copy-done = bf16[256,1152]{1,0:T(8,128)(2,1)S(1)} copy-done((bf16[256,1152]{1,0:T(8,128)(2,1)S(1)}, bf16[256,1152]{1,0:T(8,128)(2,1)}, u32[]{:S(2)}) %copy-start) | copy-done | bytes 589848
  1.7 1.1 %copy-done.1 = bf16[256,1152]{1,0:T(8,128)(2,1)S(1)} copy-done((bf16[256,1152]{1,0:T(8,128)(2,1)S(1)}, bf16[256,1152]{1,0:T(8,128)(2,1)}, u32[]{:S(2)}) %copy-start.1) | copy-done | bytes 589848
  2.8 0.4 shard_map.67
  3.1 3.5 %collective-permute-start = (bf16[256,1152]{1,0:T(8,128)(2,1)S(1)}, bf16[256,1152]{1,0:T(8,128)(2,1)S(1)}, u32[]{:S(2)}, u32[]{:S(2)}) collective-permute-start(bf16[256,1152]{1,0:T(8,128)(2,1)S(1)} %get-tuple-element.33.p0), channel_id=1, source_target_pairs={{0,8},{1,761},{2,10},{3,763},{4,12},{5,765},{6,14},{7,767},{8,16},... | collective-permute-start | bytes 1769480 | tf_op jit(solution)/shard_map/ppermute | solution.py:35
  7.9 0.8 shard_map.68
  8.8 7.4 %collective-permute-start.1 = (bf16[256,1152]{1,0:T(8,128)(2,1)S(1)}, bf16[256,1152]{1,0:T(8,128)(2,1)S(1)}, u32[]{:S(2)}, u32[]{:S(2)}) collective-permute-start(bf16[256,1152]{1,0:T(8,128)(2,1)S(1)} %get-tuple-element.37.q0), channel_id=1, source_target_pairs={{0,760},{1,9},{2,762},{3,11},{4,764},{5,13},{6,766},{7,15},{8,0},{... | collective-permute-start | bytes 1769480 | tf_op jit(solution)/shard_map/ppermute | solution.py:35
  16.2 3.8 %collective-permute-done.p1 = bf16[256,1152]{1,0:T(8,128)(2,1)S(1)} collective-permute-done((bf16[256,1152]{1,0:T(8,128)(2,1)S(1)}, bf16[256,1152]{1,0:T(8,128)(2,1)S(1)}, u32[]{:S(2)}, u32[]{:S(2)}) %collective-permute-start) | collective-permute-done | bytes 589856 | tf_op jit(solution)/shard_map/ppermute | solution.py:35
  20.0 1.9 %collective-permute-start.2 = (bf16[256,1152]{1,0:T(8,128)(2,1)S(1)}, bf16[256,1152]{1,0:T(8,128)(2,1)S(1)}, u32[]{:S(2)}, u32[]{:S(2)}) collective-permute-start(bf16[256,1152]{1,0:T(8,128)(2,1)S(1)} %collective-permute-done.p1), channel_id=1, source_target_pairs={{0,8},{1,761},{2,10},{3,763},{4,12},{5,765},{6,14},{7,767},{8,16},... | collective-permute-start | bytes 1769480 | tf_op jit(solution)/shard_map/ppermute | solution.py:35
  21.9 2.8 %collective-permute-done.1.q1 = bf16[256,1152]{1,0:T(8,128)(2,1)S(1)} collective-permute-done((bf16[256,1152]{1,0:T(8,128)(2,1)S(1)}, bf16[256,1152]{1,0:T(8,128)(2,1)S(1)}, u32[]{:S(2)}, u32[]{:S(2)}) %collective-permute-start.1) | collective-permute-done | bytes 589856 | tf_op jit(solution)/shard_map/ppermute | solution.py:35
  24.7 2.0 %shard_map.69 = (f32[24,128]{1,0:T(8,128)S(1)}, f32[256,1152]{1,0:T(8,128)S(1)}, f32[256,1152]{1,0:T(8,128)S(1)}) custom-call(f32[1]{0:T(128)S(6)} %copy.20.e_ref, f32[1]{0:T(128)S(6)} %copy.21.b_ref, f32[24,128]{1,0:T(8,128)S(1)} %get-tuple-element.36.sums_in, bf16[256,1152]{1,0:T(8,128)(2,1)S(1)} %get-tuple-element.33.p0, ...), custom_call_target="tpu_custom_call" | custom-call | flops 1000 | bytes 1000 | tf_op jit(solution)/shard_map/pallas_call | solution.py:154
  26.7 1.0 %copy-done.3 = f32[256,1152]{1,0:T(8,128)} copy-done((f32[256,1152]{1,0:T(8,128)}, f32[256,1152]{1,0:T(8,128)S(1)}, u32[]{:S(2)}) %copy-start.3) | copy-done | bytes 1179672
  27.7 1.0 %copy-done.4 = f32[256,1152]{1,0:T(8,128)} copy-done((f32[256,1152]{1,0:T(8,128)}, f32[256,1152]{1,0:T(8,128)S(1)}, u32[]{:S(2)}) %copy-start.4) | copy-done | bytes 1179672
  28.7 8.3 %collective-permute-start.3 = (bf16[256,1152]{1,0:T(8,128)(2,1)S(1)}, bf16[256,1152]{1,0:T(8,128)(2,1)S(1)}, u32[]{:S(2)}, u32[]{:S(2)}) collective-permute-start(bf16[256,1152]{1,0:T(8,128)(2,1)S(1)} %collective-permute-done.1.q1), channel_id=1, source_target_pairs={{0,760},{1,9},{2,762},{3,11},{4,764},{5,13},{6,766},{7,15},{8,0},{... | collective-permute-start | bytes 1769480 | tf_op jit(solution)/shard_map/ppermute | solution.py:35
  37.0 1.3 %shard_map.70 = f32[16,128]{1,0:T(8,128)} custom-call(f32[1]{0:T(128)S(6)} %copy.20.e_ref, f32[1]{0:T(128)S(6)} %copy.21.b_ref, f32[24,128]{1,0:T(8,128)S(1)} %get-tuple-element.42.sums_in, bf16[256,1152]{1,0:T(8,128)(2,1)S(1)} %collective-permute-done.1.q1, bf16[256,1152]{1,0:T(8,128)(2,1)S(1)} %collective-permute-done.2.p2.far2), custom_call_target="tpu_custom_call" | custom-call | flops 1000 | bytes 1000 | tf_op jit(solution)/shard_map/pallas_call | solution.py:178
  38.3 1.9 %collective-permute-start.5 = (bf16[256,1152]{1,0:T(8,128)(2,1)S(1)}, bf16[256,1152]{1,0:T(8,128)(2,1)S(1)}, u32[]{:S(2)}, u32[]{:S(2)}) collective-permute-start(bf16[256,1152]{1,0:T(8,128)(2,1)S(1)} %collective-permute-done.2.p2.far2), channel_id=1, source_target_pairs={{0,8},{1,761},{2,10},{3,763},{4,12},{5,765},{6,14},{7,767},{8,16},... | collective-permute-start | bytes 1769480 | tf_op jit(solution)/shard_map/ppermute | solution.py:35
  40.2 4.5 %all-to-all-start = ((f32[16,1,128]{2,1,0:T(1,128)}), f32[16,1,128]{2,1,0:T(1,128)S(1)}, u32[]{:S(2)}, u32[]{:S(2)}) async-start(f32[16,1,128]{2,1,0:T(1,128)} %bitcast.1), calls=%async_computation | async-start | bytes 16384 | tf_op jit(solution)/shard_map/all_to_all | solution.py:302
  44.7 0.3 collective-permute-done.3.far2
  45.0 7.3 %all-to-all-done = f32[16,1,128]{2,1,0:T(1,128)S(1)} async-done(((f32[16,1,128]{2,1,0:T(1,128)}), f32[16,1,128]{2,1,0:T(1,128)S(1)}, u32[]{:S(2)}, u32[]{:S(2)}) %all-to-all-start) | async-done | bytes 8224 | tf_op jit(solution)/shard_map/all_to_all | solution.py:302
  52.3 5.1 %collective-permute-start.4 = (bf16[256,1152]{1,0:T(8,128)(2,1)S(1)}, bf16[256,1152]{1,0:T(8,128)(2,1)}, u32[]{:S(2)}, u32[]{:S(2)}) collective-permute-start(bf16[256,1152]{1,0:T(8,128)(2,1)S(1)} %collective-permute-done.3.far2), channel_id=1, source_target_pairs={{0,760},{1,9},{2,762},{3,11},{4,764},{5,13},{6,766},{7,15},{8,0},{... | collective-permute-start | bytes 1769480 | tf_op jit(solution)/shard_map/ppermute | solution.py:35
  57.5 0.8 copy-done.5
  58.3 4.1 %shard_map.71 = (f32[256,1152]{1,0:T(8,128)}, f32[256,1152]{1,0:T(8,128)}) custom-call(f32[1]{0:T(128)S(6)} %copy.20.e_ref, f32[1]{0:T(128)S(6)} %copy.21.b_ref, bf16[256,1152]{1,0:T(8,128)(2,1)} %image.7, bf16[256,1152]{1,0:T(8,128)(2,1)} %text.7, f32[256,1152]{1,0:T(8,128)} %copy-done.3, bf16[256,1152]{1,0:T(8,128)(2,1)} %copy-done.2, ...), custom_call_target="tpu_custom_call" | custom-call | flops 1000 | bytes 1000 | tf_op jit(solution)/shard_map/pallas_call | solution.py:267
  62.4 28.9 %all_to_all.21 = f32[48,1,128]{2,1,0:T(1,128)S(1)} all-to-all(f32[48,1,128]{2,1,0:T(1,128)S(1)} %broadcast_in_dim.9), channel_id=1, replica_groups=mesh['x'=4,'l'=3,'y'=8,'h'=4,'c'=2] {'x','l','h'}, dimensions={0} | all-to-all | bytes 49152 | tf_op jit(solution)/shard_map/all_to_all | solution.py:308
  91.4 0.5 slice_reduce_fusion
  91.9 4.1 %shard_map.73 = (f32[256,1152]{1,0:T(8,128)}, f32[256,1152]{1,0:T(8,128)}) custom-call(f32[1]{0:T(128)S(6)} %copy.20.e_ref, f32[1]{0:T(128)S(6)} %copy.21.b_ref, bf16[256,1152]{1,0:T(8,128)(2,1)} %image.7, bf16[256,1152]{1,0:T(8,128)(2,1)} %text.7, f32[256,1152]{1,0:T(8,128)} %copy-done.4, ...), custom_call_target="tpu_custom_call", output_to_operand_aliasing={{0}: (7, {}), {1}: (8, {})} | custom-call | flops 1000 | bytes 1000 | tf_op jit(solution)/shard_map/pallas_call | solution.py:267
  (15 shorter events, 0.1 us)
Async XLA Ops:
  0.6 1.1 %copy-start = (bf16[256,1152]{1,0:T(8,128)(2,1)S(1)}, bf16[256,1152]{1,0:T(8,128)(2,1)}, u32[]{:S(2)}) copy-start(bf16[256,1152]{1,0:T(8,128)(2,1)} %image.7) | copy-start | bytes 1769476
  1.7 1.1 %copy-start.1 = (bf16[256,1152]{1,0:T(8,128)(2,1)S(1)}, bf16[256,1152]{1,0:T(8,128)(2,1)}, u32[]{:S(2)}) copy-start(bf16[256,1152]{1,0:T(8,128)(2,1)} %text.7) | copy-start | bytes 1769476
  3.1 16.8 %collective-permute-start = (bf16[256,1152]{1,0:T(8,128)(2,1)S(1)}, bf16[256,1152]{1,0:T(8,128)(2,1)S(1)}, u32[]{:S(2)}, u32[]{:S(2)}) collective-permute-start(bf16[256,1152]{1,0:T(8,128)(2,1)S(1)} %get-tuple-element.33.p0), channel_id=1, source_target_pairs={{0,8},{1,761},{2,10},{3,763},{4,12},{5,765},{6,14},{7,767},{8,16},... | collective-permute-start | bytes 1769480 | tf_op jit(solution)/shard_map/ppermute | solution.py:35
  8.8 15.9 %collective-permute-start.1 = (bf16[256,1152]{1,0:T(8,128)(2,1)S(1)}, bf16[256,1152]{1,0:T(8,128)(2,1)S(1)}, u32[]{:S(2)}, u32[]{:S(2)}) collective-permute-start(bf16[256,1152]{1,0:T(8,128)(2,1)S(1)} %get-tuple-element.37.q0), channel_id=1, source_target_pairs={{0,760},{1,9},{2,762},{3,11},{4,764},{5,13},{6,766},{7,15},{8,0},{... | collective-permute-start | bytes 1769480 | tf_op jit(solution)/shard_map/ppermute | solution.py:35
  20.0 17.0 %collective-permute-start.2 = (bf16[256,1152]{1,0:T(8,128)(2,1)S(1)}, bf16[256,1152]{1,0:T(8,128)(2,1)S(1)}, u32[]{:S(2)}, u32[]{:S(2)}) collective-permute-start(bf16[256,1152]{1,0:T(8,128)(2,1)S(1)} %collective-permute-done.p1), channel_id=1, source_target_pairs={{0,8},{1,761},{2,10},{3,763},{4,12},{5,765},{6,14},{7,767},{8,16},... | collective-permute-start | bytes 1769480 | tf_op jit(solution)/shard_map/ppermute | solution.py:35
  26.6 1.0 %copy-start.3 = (f32[256,1152]{1,0:T(8,128)}, f32[256,1152]{1,0:T(8,128)S(1)}, u32[]{:S(2)}) copy-start(f32[256,1152]{1,0:T(8,128)S(1)} %get-tuple-element.46.near) | copy-start | bytes 3538948
  27.7 1.0 %copy-start.4 = (f32[256,1152]{1,0:T(8,128)}, f32[256,1152]{1,0:T(8,128)S(1)}, u32[]{:S(2)}) copy-start(f32[256,1152]{1,0:T(8,128)S(1)} %get-tuple-element.40.near) | copy-start | bytes 3538948
  28.7 16.3 %collective-permute-start.3 = (bf16[256,1152]{1,0:T(8,128)(2,1)S(1)}, bf16[256,1152]{1,0:T(8,128)(2,1)S(1)}, u32[]{:S(2)}, u32[]{:S(2)}) collective-permute-start(bf16[256,1152]{1,0:T(8,128)(2,1)S(1)} %collective-permute-done.1.q1), channel_id=1, source_target_pairs={{0,760},{1,9},{2,762},{3,11},{4,764},{5,13},{6,766},{7,15},{8,0},{... | collective-permute-start | bytes 1769480 | tf_op jit(solution)/shard_map/ppermute | solution.py:35
  37.0 20.5 %copy-start.2 = (bf16[256,1152]{1,0:T(8,128)(2,1)}, bf16[256,1152]{1,0:T(8,128)(2,1)S(1)}, u32[]{:S(2)}) copy-start(bf16[256,1152]{1,0:T(8,128)(2,1)S(1)} %collective-permute-done.2.p2.far2) | copy-start | bytes 1769476
  38.3 19.2 %collective-permute-start.5 = (bf16[256,1152]{1,0:T(8,128)(2,1)S(1)}, bf16[256,1152]{1,0:T(8,128)(2,1)S(1)}, u32[]{:S(2)}, u32[]{:S(2)}) collective-permute-start(bf16[256,1152]{1,0:T(8,128)(2,1)S(1)} %collective-permute-done.2.p2.far2), channel_id=1, source_target_pairs={{0,8},{1,761},{2,10},{3,763},{4,12},{5,765},{6,14},{7,767},{8,16},... | collective-permute-start | bytes 1769480 | tf_op jit(solution)/shard_map/ppermute | solution.py:35
  40.2 12.1 %all-to-all-start = ((f32[16,1,128]{2,1,0:T(1,128)}), f32[16,1,128]{2,1,0:T(1,128)S(1)}, u32[]{:S(2)}, u32[]{:S(2)}) async-start(f32[16,1,128]{2,1,0:T(1,128)} %bitcast.1), calls=%async_computation | async-start | bytes 16384 | tf_op jit(solution)/shard_map/all_to_all | solution.py:302
  45.0 46.4 %copy-start.6 = (bf16[256,1152]{1,0:T(8,128)(2,1)}, bf16[256,1152]{1,0:T(8,128)(2,1)S(1)}, u32[]{:S(2)}) copy-start(bf16[256,1152]{1,0:T(8,128)(2,1)S(1)} %collective-permute-done.3.far2) | copy-start | bytes 1769476
  52.3 39.6 %collective-permute-start.4 = (bf16[256,1152]{1,0:T(8,128)(2,1)S(1)}, bf16[256,1152]{1,0:T(8,128)(2,1)}, u32[]{:S(2)}, u32[]{:S(2)}) collective-permute-start(bf16[256,1152]{1,0:T(8,128)(2,1)S(1)} %collective-permute-done.3.far2), channel_id=1, source_target_pairs={{0,760},{1,9},{2,762},{3,11},{4,764},{5,13},{6,766},{7,15},{8,0},{... | collective-permute-start | bytes 1769480 | tf_op jit(solution)/shard_map/ppermute | solution.py:35
  57.5 0.8 copy-start.5

commit v6 on v5

--- a/solution.py
+++ b/solution.py
@@ -235,41 +235,57 @@
     return from_text
 
 
-def side_kernel(side, when, e_ref, b_ref, image, text, near, far2, far3, *refs):
-    out_image, out_text, total, raw, out, own, far, d, sems, out_sem = refs if when == "early" else refs[2:]
+def unit_rows(raw, own):
+    for r in range(0, ROWS, CHUNK):
+        v = raw[r : r + CHUNK, :].astype(F32)
+        own[r : r + CHUNK, :] = (v * inverse_norm(v)).astype(BF16)
+
+
+def q_kernel(when, e_ref, b_ref, image, text, g_q, p2, p3, g_p, q2, *refs):
+    out_image, out_text, out_p, total, raw, out, own, far, d, total_p, raw_p, far_p, sems, out_sems = (
+        refs if when == "early" else refs[3:]
+    )
     early = 3 * lax.axis_index("h") + lax.axis_index("l") < EARLY_PLANES
-    is_text = lax.axis_index("c") == 1 - side
-
-    def work():
-        raw_copy = load_raw(is_text, image, text, raw, sems.at[3])
-        copies = started([(far2, far.at[pl.ds(0, ROWS), :]), (far3, far.at[pl.ds(ROWS, ROWS), :]), (near, total)], sems)
+    q_text = lax.axis_index("c") == 1
+    p_text = lax.axis_index("c") == 0
+
+    @pl.when(early if when == "early" else jnp.logical_not(early))
+    def _():
+        raw_copy = load_raw(q_text, image, text, raw, sems.at[5])
+        copies = started(
+            [(p2, far.at[pl.ds(0, ROWS), :]), (p3, far.at[pl.ds(ROWS, ROWS), :]), (g_q, total), (q2, far_p), (g_p, total_p)],
+            sems,
+        )
+        raw_p_copy = load_raw(p_text, image, text, raw_p, sems.at[6])
         raw_copy.wait()
-        for r in range(0, ROWS, CHUNK):
-            v = raw[r : r + CHUNK, :].astype(F32)
-            own[r : r + CHUNK, :] = (v * inverse_norm(v)).astype(BF16)
+        unit_rows(raw, own)
         for n in range(2):
             copies[n].wait()
             rows = pl.ds(n * ROWS, ROWS)
             d[:, rows] = slope_block(e_ref, b_ref, own[...], far[rows, :])
         copies[2].wait()
         total[...] += jnp.dot(d[...], far[...], preferred_element_type=F32)
-        finish(e_ref, total, raw, out, is_text, out_image, out_text, out_sem)
-        pltpu.make_async_copy(out, out_text, out_sem).wait()
-
-    if when == "always":
-        work()
-    else:
-        pl.when(early if when == "early" else jnp.logical_not(early))(work)
-
-
-def one_side(side, when, args, previous=()):
+        finish(e_ref, total, raw, out, q_text, out_image, out_text, out_sems.at[0])
+        raw_p_copy.wait()
+        unit_rows(raw_p, own)
+        copies[3].wait()
+        slopes = slope_block(e_ref, b_ref, own[...], far_p[...])
+        copies[4].wait()
+        total_p[...] += jnp.dot(slopes, far_p[...], preferred_element_type=F32)
+        store = pltpu.make_async_copy(total_p, out_p, out_sems.at[1])
+        store.start()
+        store.wait()
+        pltpu.make_async_copy(out, out_text, out_sems.at[0]).wait()
+
+
+def q_side(when, args, previous=()):
     n = len(args)
     return pl.pallas_call(
-        functools.partial(side_kernel, side, when),
-        out_shape=(GRAD, GRAD),
+        functools.partial(q_kernel, when),
+        out_shape=(GRAD, GRAD, GRAD),
         in_specs=[SMEM, SMEM] + [HBM] * (n - 2 + len(previous)),
-        out_specs=(HBM, HBM),
-        input_output_aliases={n: 0, n + 1: 1} if previous else {},
+        out_specs=(HBM, HBM, HBM),
+        input_output_aliases={n: 0, n + 1: 1, n + 2: 2} if previous else {},
         scratch_shapes=[
             pltpu.VMEM((ROWS, D), F32),
             pltpu.VMEM((ROWS, D), BF16),
@@ -277,7 +293,47 @@
             pltpu.VMEM((ROWS, D), BF16),
             pltpu.VMEM((2 * ROWS, D), BF16),
             pltpu.VMEM((ROWS, 2 * ROWS), BF16),
-            pltpu.SemaphoreType.DMA((4,)),
+            pltpu.VMEM((ROWS, D), F32),
+            pltpu.VMEM((ROWS, D), BF16),
+            pltpu.VMEM((ROWS, D), BF16),
+            pltpu.SemaphoreType.DMA((7,)),
+            pltpu.SemaphoreType.DMA((2,)),
+        ],
+        compiler_params=WHOLE,
+        cost_estimate=LIGHT,
+    )(*args, *previous)
+
+
+def p_kernel(e_ref, b_ref, image, text, g_p, q3, *refs):
+    _, _, out_image, out_text, total, raw, out, own, far, sems, out_sem = refs
+    is_text = lax.axis_index("c") == 0
+    raw_copy = load_raw(is_text, image, text, raw, sems.at[2])
+    copies = started([(q3, far), (g_p, total)], sems)
+    raw_copy.wait()
+    unit_rows(raw, own)
+    copies[0].wait()
+    slopes = slope_block(e_ref, b_ref, own[...], far[...])
+    copies[1].wait()
+    total[...] += jnp.dot(slopes, far[...], preferred_element_type=F32)
+    finish(e_ref, total, raw, out, is_text, out_image, out_text, out_sem)
+    pltpu.make_async_copy(out, out_text, out_sem).wait()
+
+
+def p_side(args, previous):
+    n = len(args)
+    return pl.pallas_call(
+        p_kernel,
+        out_shape=(GRAD, GRAD),
+        in_specs=[SMEM, SMEM] + [HBM] * n,
+        out_specs=(HBM, HBM),
+        input_output_aliases={n: 0, n + 1: 1},
+        scratch_shapes=[
+            pltpu.VMEM((ROWS, D), F32),
+            pltpu.VMEM((ROWS, D), BF16),
+            pltpu.VMEM((ROWS, D), F32),
+            pltpu.VMEM((ROWS, D), BF16),
+            pltpu.VMEM((ROWS, D), BF16),
+            pltpu.SemaphoreType.DMA((3,)),
             pltpu.SemaphoreType.DMA,
         ],
         compiler_params=WHOLE,
@@ -303,13 +359,13 @@
     row, q2 = bar((row, q2))
     q3 = hop(q2, -1)
     row, p3 = bar((jnp.sum(row, axis=0, keepdims=True), p3))
-    q_args = (e, b, image, text, g_q, p2, p3)
-    row, done = bar((row, one_side(0, "early", q_args)))
+    q_args = (e, b, image, text, g_q, p2, p3, g_p, q2)
+    row, done = bar((row, q_side("early", q_args)))
     row = lax.all_to_all(jnp.broadcast_to(row, (48, 128)), ("x", "l", "h"), 0, 0, tiled=True)
     row, done = bar((row, done))
     totals = jnp.sum(row[:, :3], axis=0)
-    done = one_side(0, "late", q_args, done)
-    grad_image, grad_text = one_side(1, "always", (e, b, image, text, g_p, q2, q3), done)
+    grad_image, grad_text, g_p = q_side("late", q_args, done)
+    grad_image, grad_text = p_side((e, b, image, text, g_p, q3), (grad_image, grad_text))
     return grad_image, grad_text, totals
 
 

time: 96.5 us -> 97.3 us (level)
  transfers between devices with their start and end apart: 7 -> 7, of which waited for: 4 -> 4; matrix products, arithmetic and copies ran while one was open for 1% -> 1% of each run, Pallas kernels for 9% -> 10%
where the time goes in v6:
time: 97.3 us; the launch traced here: 96.8 us
  starting transfers between devices  32.6 us (34%)
  blocking collectives  28.9 us (30%)
  waiting for transfers between devices  14.2 us (15%)
  Pallas kernels  13.5 us (14%)
  local copies, waits for them, and re-layouts  5 us (5%)
  between operations  2.09 us (2%)
    all_to_all x1, blocking collectives, body(): lax.all_to_all(jnp.broadcast_to(row, (48, 128)), ('x', 'l', 'h'), 0, 0, t...  28.9 us
    ppermute x6, starting transfers between devices, hop(): return lax.ppermute(value, AXES, pairs)  28.1 us
    all_to_all x1, waiting for transfers between devices, body(): row = lax.all_to_all(row, ('y', 'c'), 0, 0, tiled=True)  7.39 us
    ppermute x6, waiting for transfers between devices, hop(): return lax.ppermute(value, AXES, pairs)  6.82 us
    pallas_call x2, Pallas kernels, q_side(): pl.pallas_call(functools.partial(q_kernel, when), out_shape=(GRAD, GRAD,...  5.58 us
    unnamed x14, local copies, waits for them, and re-layouts  4.98 us
    all_to_all x1, starting transfers between devices, body(): row = lax.all_to_all(row, ('y', 'c'), 0, 0, tiled=True)  4.53 us
    pallas_call x1, Pallas kernels, p_side(): pl.pallas_call(p_kernel, out_shape=(GRAD, GRAD), in_specs=[SMEM, SMEM] +...  3.46 us
  transfers between devices with their start and end apart: 7, of which 4 were waited for; matrix products, arithmetic and copies ran while one was open for 1% of the time, Pallas kernels for 10%

profile of v6, /device:TPU:2, one launch (start us, length us, event | category | flops | bytes accessed | tf_op | source)
XLA Modules:
  0.0 96.8 jit_solution(17678427509221639788)
XLA Ops:
  0.6 1.1 %copy-done = bf16[256,1152]{1,0:T(8,128)(2,1)S(1)} copy-done((bf16[256,1152]{1,0:T(8,128)(2,1)S(1)}, bf16[256,1152]{1,0:T(8,128)(2,1)}, u32[]{:S(2)}) %copy-start) | copy-done | bytes 589848
  1.7 1.1 %copy-done.1 = bf16[256,1152]{1,0:T(8,128)(2,1)S(1)} copy-done((bf16[256,1152]{1,0:T(8,128)(2,1)S(1)}, bf16[256,1152]{1,0:T(8,128)(2,1)}, u32[]{:S(2)}) %copy-start.1) | copy-done | bytes 589848
  2.8 0.4 shard_map.67
  3.1 3.5 %collective-permute-start = (bf16[256,1152]{1,0:T(8,128)(2,1)S(1)}, bf16[256,1152]{1,0:T(8,128)(2,1)S(1)}, u32[]{:S(2)}, u32[]{:S(2)}) collective-permute-start(bf16[256,1152]{1,0:T(8,128)(2,1)S(1)} %get-tuple-element.37.p0), channel_id=1, source_target_pairs={{0,8},{1,761},{2,10},{3,763},{4,12},{5,765},{6,14},{7,767},{8,16},... | collective-permute-start | bytes 1769480 | tf_op jit(solution)/shard_map/ppermute | solution.py:35
  7.9 0.8 shard_map.68
  8.8 7.4 %collective-permute-start.1 = (bf16[256,1152]{1,0:T(8,128)(2,1)S(1)}, bf16[256,1152]{1,0:T(8,128)(2,1)S(1)}, u32[]{:S(2)}, u32[]{:S(2)}) collective-permute-start(bf16[256,1152]{1,0:T(8,128)(2,1)S(1)} %get-tuple-element.41.q0), channel_id=1, source_target_pairs={{0,760},{1,9},{2,762},{3,11},{4,764},{5,13},{6,766},{7,15},{8,0},{... | collective-permute-start | bytes 1769480 | tf_op jit(solution)/shard_map/ppermute | solution.py:35
  16.2 3.8 %collective-permute-done.p1 = bf16[256,1152]{1,0:T(8,128)(2,1)S(1)} collective-permute-done((bf16[256,1152]{1,0:T(8,128)(2,1)S(1)}, bf16[256,1152]{1,0:T(8,128)(2,1)S(1)}, u32[]{:S(2)}, u32[]{:S(2)}) %collective-permute-start) | collective-permute-done | bytes 589856 | tf_op jit(solution)/shard_map/ppermute | solution.py:35
  20.0 1.9 %collective-permute-start.2 = (bf16[256,1152]{1,0:T(8,128)(2,1)S(1)}, bf16[256,1152]{1,0:T(8,128)(2,1)S(1)}, u32[]{:S(2)}, u32[]{:S(2)}) collective-permute-start(bf16[256,1152]{1,0:T(8,128)(2,1)S(1)} %collective-permute-done.p1), channel_id=1, source_target_pairs={{0,8},{1,761},{2,10},{3,763},{4,12},{5,765},{6,14},{7,767},{8,16},... | collective-permute-start | bytes 1769480 | tf_op jit(solution)/shard_map/ppermute | solution.py:35
  21.9 2.8 %collective-permute-done.1.q1 = bf16[256,1152]{1,0:T(8,128)(2,1)S(1)} collective-permute-done((bf16[256,1152]{1,0:T(8,128)(2,1)S(1)}, bf16[256,1152]{1,0:T(8,128)(2,1)S(1)}, u32[]{:S(2)}, u32[]{:S(2)}) %collective-permute-start.1) | collective-permute-done | bytes 589856 | tf_op jit(solution)/shard_map/ppermute | solution.py:35
  24.7 2.0 %shard_map.69 = (f32[24,128]{1,0:T(8,128)S(1)}, f32[256,1152]{1,0:T(8,128)S(1)}, f32[256,1152]{1,0:T(8,128)S(1)}) custom-call(f32[1]{0:T(128)S(6)} %copy.22.e_ref, f32[1]{0:T(128)S(6)} %copy.23.b_ref, f32[24,128]{1,0:T(8,128)S(1)} %get-tuple-element.40.sums_in, bf16[256,1152]{1,0:T(8,128)(2,1)S(1)} %get-tuple-element.37.p0, ...), custom_call_target="tpu_custom_call" | custom-call | flops 1000 | bytes 1000 | tf_op jit(solution)/shard_map/pallas_call | solution.py:154
  26.6 1.0 %copy-done.3 = f32[256,1152]{1,0:T(8,128)} copy-done((f32[256,1152]{1,0:T(8,128)}, f32[256,1152]{1,0:T(8,128)S(1)}, u32[]{:S(2)}) %copy-start.3) | copy-done | bytes 1179672
  27.7 1.0 %copy-done.4 = f32[256,1152]{1,0:T(8,128)} copy-done((f32[256,1152]{1,0:T(8,128)}, f32[256,1152]{1,0:T(8,128)S(1)}, u32[]{:S(2)}) %copy-start.4) | copy-done | bytes 1179672
  28.7 8.3 %collective-permute-start.3 = (bf16[256,1152]{1,0:T(8,128)(2,1)S(1)}, bf16[256,1152]{1,0:T(8,128)(2,1)S(1)}, u32[]{:S(2)}, u32[]{:S(2)}) collective-permute-start(bf16[256,1152]{1,0:T(8,128)(2,1)S(1)} %collective-permute-done.1.q1), channel_id=1, source_target_pairs={{0,760},{1,9},{2,762},{3,11},{4,764},{5,13},{6,766},{7,15},{8,0},{... | collective-permute-start | bytes 1769480 | tf_op jit(solution)/shard_map/ppermute | solution.py:35
  37.0 1.3 %shard_map.70 = f32[16,128]{1,0:T(8,128)} custom-call(f32[1]{0:T(128)S(6)} %copy.22.e_ref, f32[1]{0:T(128)S(6)} %copy.23.b_ref, f32[24,128]{1,0:T(8,128)S(1)} %get-tuple-element.46.sums_in, bf16[256,1152]{1,0:T(8,128)(2,1)S(1)} %collective-permute-done.1.q1, bf16[256,1152]{1,0:T(8,128)(2,1)S(1)} %collective-permute-done.2.p2), custom_call_target="tpu_custom_call" | custom-call | flops 1000 | bytes 1000 | tf_op jit(solution)/shard_map/pallas_call | solution.py:178
  38.3 1.9 %collective-permute-start.4 = (bf16[256,1152]{1,0:T(8,128)(2,1)S(1)}, bf16[256,1152]{1,0:T(8,128)(2,1)S(1)}, u32[]{:S(2)}, u32[]{:S(2)}) collective-permute-start(bf16[256,1152]{1,0:T(8,128)(2,1)S(1)} %collective-permute-done.2.p2), channel_id=1, source_target_pairs={{0,8},{1,761},{2,10},{3,763},{4,12},{5,765},{6,14},{7,767},{8,16},... | collective-permute-start | bytes 1769480 | tf_op jit(solution)/shard_map/ppermute | solution.py:35
  40.2 4.5 %all-to-all-start = ((f32[16,1,128]{2,1,0:T(1,128)}), f32[16,1,128]{2,1,0:T(1,128)S(1)}, u32[]{:S(2)}, u32[]{:S(2)}) async-start(f32[16,1,128]{2,1,0:T(1,128)} %bitcast.1), calls=%async_computation | async-start | bytes 16384 | tf_op jit(solution)/shard_map/all_to_all | solution.py:358
  44.7 0.2 collective-permute-done.3.q2
  45.0 7.4 %all-to-all-done = f32[16,1,128]{2,1,0:T(1,128)S(1)} async-done(((f32[16,1,128]{2,1,0:T(1,128)}), f32[16,1,128]{2,1,0:T(1,128)S(1)}, u32[]{:S(2)}, u32[]{:S(2)}) %all-to-all-start) | async-done | bytes 8224 | tf_op jit(solution)/shard_map/all_to_all | solution.py:358
  52.3 5.1 %collective-permute-start.5 = (bf16[256,1152]{1,0:T(8,128)(2,1)S(1)}, bf16[256,1152]{1,0:T(8,128)(2,1)}, u32[]{:S(2)}, u32[]{:S(2)}) collective-permute-start(bf16[256,1152]{1,0:T(8,128)(2,1)S(1)} %collective-permute-done.3.q2), channel_id=1, source_target_pairs={{0,760},{1,9},{2,762},{3,11},{4,764},{5,13},{6,766},{7,15},{8,0},{... | collective-permute-start | bytes 1769480 | tf_op jit(solution)/shard_map/ppermute | solution.py:35
  57.5 0.8 copy-done.6
  58.3 5.5 %shard_map.71 = (f32[256,1152]{1,0:T(8,128)}, f32[256,1152]{1,0:T(8,128)}, f32[256,1152]{1,0:T(8,128)}) custom-call(f32[1]{0:T(128)S(6)} %copy.22.e_ref, f32[1]{0:T(128)S(6)} %copy.23.b_ref, bf16[256,1152]{1,0:T(8,128)(2,1)} %image.7, bf16[256,1152]{1,0:T(8,128)(2,1)} %text.7, f32[256,1152]{1,0:T(8,128)} %copy-done.3, bf16[256,1152]{1,0:T(8,128)(2,1)} %copy-done.2, ...), custom_call_target="tpu_custom_call" | custom-call | flops 1000 | bytes 1000 | tf_op jit(solution)/shard_map/pallas_call | solution.py:283
  63.8 28.9 %all_to_all.21 = f32[48,1,128]{2,1,0:T(1,128)S(1)} all-to-all(f32[48,1,128]{2,1,0:T(1,128)S(1)} %broadcast_in_dim.9), channel_id=1, replica_groups=mesh['x'=4,'l'=3,'y'=8,'h'=4,'c'=2] {'x','l','h'}, dimensions={0} | all-to-all | bytes 49152 | tf_op jit(solution)/shard_map/all_to_all | solution.py:364
  92.8 0.5 slice_reduce_fusion
  93.4 3.5 %shard_map.73 = (f32[256,1152]{1,0:T(8,128)}, f32[256,1152]{1,0:T(8,128)}) custom-call(f32[1]{0:T(128)S(6)} %copy.22.e_ref, f32[1]{0:T(128)S(6)} %copy.23.b_ref, bf16[256,1152]{1,0:T(8,128)(2,1)} %image.7, bf16[256,1152]{1,0:T(8,128)(2,1)} %text.7, f32[256,1152]{1,0:T(8,128)} %get-tuple-element.65.g_p, ...), custom_call_target="tpu_custom_call", output_to_operand_aliasing={{0}: (6, {}), {1}: (7, {})} | custom-call | flops 1000 | bytes 1000 | tf_op jit(solution)/shard_map/pallas_call | solution.py:324
  (15 shorter events, 0.1 us)
Async XLA Ops:
  0.6 1.1 %copy-start = (bf16[256,1152]{1,0:T(8,128)(2,1)S(1)}, bf16[256,1152]{1,0:T(8,128)(2,1)}, u32[]{:S(2)}) copy-start(bf16[256,1152]{1,0:T(8,128)(2,1)} %image.7) | copy-start | bytes 1769476
  1.7 1.1 %copy-start.1 = (bf16[256,1152]{1,0:T(8,128)(2,1)S(1)}, bf16[256,1152]{1,0:T(8,128)(2,1)}, u32[]{:S(2)}) copy-start(bf16[256,1152]{1,0:T(8,128)(2,1)} %text.7) | copy-start | bytes 1769476
  3.1 16.8 %collective-permute-start = (bf16[256,1152]{1,0:T(8,128)(2,1)S(1)}, bf16[256,1152]{1,0:T(8,128)(2,1)S(1)}, u32[]{:S(2)}, u32[]{:S(2)}) collective-permute-start(bf16[256,1152]{1,0:T(8,128)(2,1)S(1)} %get-tuple-element.37.p0), channel_id=1, source_target_pairs={{0,8},{1,761},{2,10},{3,763},{4,12},{5,765},{6,14},{7,767},{8,16},... | collective-permute-start | bytes 1769480 | tf_op jit(solution)/shard_map/ppermute | solution.py:35
  8.8 15.9 %collective-permute-start.1 = (bf16[256,1152]{1,0:T(8,128)(2,1)S(1)}, bf16[256,1152]{1,0:T(8,128)(2,1)S(1)}, u32[]{:S(2)}, u32[]{:S(2)}) collective-permute-start(bf16[256,1152]{1,0:T(8,128)(2,1)S(1)} %get-tuple-element.41.q0), channel_id=1, source_target_pairs={{0,760},{1,9},{2,762},{3,11},{4,764},{5,13},{6,766},{7,15},{8,0},{... | collective-permute-start | bytes 1769480 | tf_op jit(solution)/shard_map/ppermute | solution.py:35
  20.0 17.0 %collective-permute-start.2 = (bf16[256,1152]{1,0:T(8,128)(2,1)S(1)}, bf16[256,1152]{1,0:T(8,128)(2,1)S(1)}, u32[]{:S(2)}, u32[]{:S(2)}) collective-permute-start(bf16[256,1152]{1,0:T(8,128)(2,1)S(1)} %collective-permute-done.p1), channel_id=1, source_target_pairs={{0,8},{1,761},{2,10},{3,763},{4,12},{5,765},{6,14},{7,767},{8,16},... | collective-permute-start | bytes 1769480 | tf_op jit(solution)/shard_map/ppermute | solution.py:35
  26.6 1.0 %copy-start.3 = (f32[256,1152]{1,0:T(8,128)}, f32[256,1152]{1,0:T(8,128)S(1)}, u32[]{:S(2)}) copy-start(f32[256,1152]{1,0:T(8,128)S(1)} %get-tuple-element.44.g_q) | copy-start | bytes 3538948
  27.7 1.0 %copy-start.4 = (f32[256,1152]{1,0:T(8,128)}, f32[256,1152]{1,0:T(8,128)S(1)}, u32[]{:S(2)}) copy-start(f32[256,1152]{1,0:T(8,128)S(1)} %get-tuple-element.52.g_p) | copy-start | bytes 3538948
  28.7 16.3 %collective-permute-start.3 = (bf16[256,1152]{1,0:T(8,128)(2,1)S(1)}, bf16[256,1152]{1,0:T(8,128)(2,1)S(1)}, u32[]{:S(2)}, u32[]{:S(2)}) collective-permute-start(bf16[256,1152]{1,0:T(8,128)(2,1)S(1)} %collective-permute-done.1.q1), channel_id=1, source_target_pairs={{0,760},{1,9},{2,762},{3,11},{4,764},{5,13},{6,766},{7,15},{8,0},{... | collective-permute-start | bytes 1769480 | tf_op jit(solution)/shard_map/ppermute | solution.py:35
  37.0 20.5 %copy-start.2 = (bf16[256,1152]{1,0:T(8,128)(2,1)}, bf16[256,1152]{1,0:T(8,128)(2,1)S(1)}, u32[]{:S(2)}) copy-start(bf16[256,1152]{1,0:T(8,128)(2,1)S(1)} %collective-permute-done.2.p2) | copy-start | bytes 1769476
  38.3 19.2 %collective-permute-start.4 = (bf16[256,1152]{1,0:T(8,128)(2,1)S(1)}, bf16[256,1152]{1,0:T(8,128)(2,1)S(1)}, u32[]{:S(2)}, u32[]{:S(2)}) collective-permute-start(bf16[256,1152]{1,0:T(8,128)(2,1)S(1)} %collective-permute-done.2.p2), channel_id=1, source_target_pairs={{0,8},{1,761},{2,10},{3,763},{4,12},{5,765},{6,14},{7,767},{8,16},... | collective-permute-start | bytes 1769480 | tf_op jit(solution)/shard_map/ppermute | solution.py:35
  40.2 12.2 %all-to-all-start = ((f32[16,1,128]{2,1,0:T(1,128)}), f32[16,1,128]{2,1,0:T(1,128)S(1)}, u32[]{:S(2)}, u32[]{:S(2)}) async-start(f32[16,1,128]{2,1,0:T(1,128)} %bitcast.1), calls=%async_computation | async-start | bytes 16384 | tf_op jit(solution)/shard_map/all_to_all | solution.py:358
  44.9 12.6 %copy-start.5 = (bf16[256,1152]{1,0:T(8,128)(2,1)}, bf16[256,1152]{1,0:T(8,128)(2,1)S(1)}, u32[]{:S(2)}) copy-start(bf16[256,1152]{1,0:T(8,128)(2,1)S(1)} %collective-permute-done.3.q2) | copy-start | bytes 1769476
  52.3 41.0 %collective-permute-start.5 = (bf16[256,1152]{1,0:T(8,128)(2,1)S(1)}, bf16[256,1152]{1,0:T(8,128)(2,1)}, u32[]{:S(2)}, u32[]{:S(2)}) collective-permute-start(bf16[256,1152]{1,0:T(8,128)(2,1)S(1)} %collective-permute-done.3.q2), channel_id=1, source_target_pairs={{0,760},{1,9},{2,762},{3,11},{4,764},{5,13},{6,766},{7,15},{8,0},{... | collective-permute-start | bytes 1769480 | tf_op jit(solution)/shard_map/ppermute | solution.py:35
  57.5 0.8 copy-start.6
